TPU v7x, 32 devices: a whole 2x2x4 slice. The times are simulated.
32 devices in a mesh: roll: 4 (over x, core), mach: 2 (over y), cross: 4 (over z).
Axes of the slice: x: 2, y: 2, z: 4, core: 2. Of those that a mesh axis runs over, the one named last changes fastest.
Arguments:
- density: bfloat16 [128, 4096, 2048], P('roll', 'mach', 'cross'), may hold values from 0 to 1
- roll_start: float32 [32, 128], P(None, 'roll'), may hold values from 0.05 to 1
- mach_factor: bfloat16 [32, 4096], P(None, 'mach'), may hold values from 0.0099487305 to 1
- cross_factor: bfloat16 [32, 2048], P(None, 'cross'), may hold values from 0.0099487305 to 1
Outputs:
- roll_factor: float32 [32, 128], P(None, 'roll')
- mode_two: float32 [32, 4096], P(None, ('mach', 'cross'))
All inputs are finite; a program needn't handle non-finite values.
Results may differ from a plain program's by a relative error of at most 0.0003.
Values sent between devices are 32-bit elements; how exact they have to be, the bound alone decides.
No kernel may reach another device: no remote copies, remote signals or barrier semaphores. Data moves between devices by JAX's collectives and lax.ppermute only.
A program may use at most 128 MiB of HBM per device.

v0:
```python
import jax
import jax.numpy as jnp
from jax import lax
from jax.sharding import PartitionSpec as P


def hals_rows(roll_rows, mttkrp, gram):

    def column_step(column, rows):
        column = jnp.asarray(column).astype(jnp.int32)
        gram_row = lax.dynamic_slice_in_dim(gram, column, 1, 0)
        diag_entry = lax.dynamic_slice_in_dim(gram_row, column, 1, 1)
        current = lax.dynamic_slice_in_dim(rows, column, 1, 0)
        target = lax.dynamic_slice_in_dim(mttkrp, column, 1, 0)
        mixed = jnp.dot(gram_row, rows, precision=lax.Precision.HIGHEST)
        updated = jnp.maximum(current + (target - mixed) / diag_entry, 0.0)
        return lax.dynamic_update_slice_in_dim(rows, updated, column, 0)

    return lax.fori_loop(0, roll_rows.shape[0], column_step, roll_rows)


def local(density, roll_start, mach_factor, cross_factor):
    rolls_here, bins_here, cross_here = density.shape
    rank = cross_factor.shape[0]
    flat = density.reshape(rolls_here * bins_here, cross_here)
    partial_value = lax.dot_general(
        cross_factor, flat, (((1,), (1,)), ((), ())), preferred_element_type=jnp.float32
    )
    partial_value = partial_value.reshape(rank, rolls_here, bins_here)
    local_terms = jnp.einsum(
        "rij,rj->ri",
        partial_value,
        mach_factor.astype(jnp.float32),
        precision=lax.Precision.HIGHEST,
    )
    local_mach = jnp.dot(mach_factor, mach_factor.T, preferred_element_type=jnp.float32)
    local_cross = jnp.dot(cross_factor, cross_factor.T, preferred_element_type=jnp.float32)
    mttkrp = lax.psum(local_terms, ("mach", "cross"))
    gram_mach = lax.psum(local_mach, "mach")
    gram_cross = lax.psum(local_cross, "cross")
    gram = gram_mach * gram_cross
    roll_factor = hals_rows(roll_start, mttkrp, gram)
    term = jnp.einsum("rij,ri->rj", partial_value, roll_factor, precision=lax.Precision.HIGHEST)
    whole = lax.psum(term, ("roll", "cross"))
    span = whole.shape[1] // lax.axis_size("cross")
    total = lax.dynamic_slice_in_dim(whole, lax.axis_index("cross") * span, span, 1)
    all_rolls = rolls_here * lax.axis_size("roll")
    all_cross = cross_here * lax.axis_size("cross")
    scale = rank / (all_rolls * all_cross)
    mode_two = total * scale
    return (roll_factor, mode_two)


def solution(mesh):
    in_specs = (P("roll", "mach", "cross"), P(None, "roll"), P(None, "mach"), P(None, "cross"))
    out_specs = (P(None, "roll"), P(None, ("mach", "cross")))
    return jax.shard_map(local, mesh=mesh, in_specs=in_specs, out_specs=out_specs, check_vma=False)
```

profile of v0, /device:TPU:0, one launch (start us, length us, event | category | flops | bytes accessed | tf_op | source)
XLA Modules:
  0.0 266.0 jit_solution(5635341677431458956)
XLA Ops:
  7.2 1.0 fusion.13
  8.2 30.2 %fusion.10 = f32[32,32,2048]{2,0,1:T(8,128)} fusion(bf16[32,2048,512]{2,1,0:T(8,128)(2,1)} %param.6, bf16[32,512]{1,0:T(8,128)(2,1)} %param.9), kind=kOutput, calls=%fused_computation.15 | convolution fusion | flops 2147483648 | bytes 75530240 | tf_op jit(solution)/shard_map/dot_general | solution.py:26
  38.5 11.7 %fusion.7 = f32[32,1,32]{2,1,0:T(1,128)S(1)} fusion(f32[32,32,2048]{2,0,1:T(8,128)} %fusion.10, bf16[32,2048,1]{1,0,2:T(8,128)(2,1)S(1)} %bitcast.31), kind=kOutput, calls=%fused_computation.10 | convolution fusion | flops 25165824 | bytes 8523776 | tf_op jit(solution)/shard_map/rij,rj->ri/dot_general | solution.py:30
  50.3 39.1 %psum.28 = f32[32,32]{1,0:T(8,128)S(1)} all-reduce(f32[32,32]{1,0:T(8,128)S(1)} %bitcast.34), channel_id=1, replica_groups=mesh['roll'=4,'mach'=2,'cross'=4] {'mach','cross'}, use_global_device_ids=true, to_apply=%region_2.0 | all-reduce | flops 1024 | bytes 8192 | tf_op jit(solution)/shard_map/psum | solution.py:38
  89.3 7.1 %psum.29 = f32[32,32]{1,0:T(8,128)S(1)} all-reduce(f32[32,32]{1,0:T(8,128)S(1)} %fusion.12), channel_id=1, replica_groups=mesh['roll'=4,'mach'=2,'cross'=4] {'mach'}, use_global_device_ids=true, to_apply=%region_0.0 | all-reduce | flops 1024 | bytes 8192 | tf_op jit(solution)/shard_map/psum | solution.py:39
  96.4 15.7 %psum.30 = f32[32,32]{1,0:T(8,128)S(1)} all-reduce(f32[32,32]{1,0:T(8,128)S(1)} %fusion.13), channel_id=1, replica_groups=mesh['roll'=4,'mach'=2,'cross'=4] {'cross'}, use_global_device_ids=true, to_apply=%region_1.0 | all-reduce | flops 1024 | bytes 8192 | tf_op jit(solution)/shard_map/psum | solution.py:40
  112.1 45.2 %while.16 = (s32[]{:T(128)}, f32[32,32]{1,0:T(8,128)S(1)}, f32[32,32]{1,0:T(8,128)S(1)}, f32[32,32]{1,0:T(8,128)S(1)}, s32[]{:T(128)}, /*index=5*/s32[]{:T(128)}, s32[]{:T(128)}) while((s32[]{:T(128)}, f32[32,32]{1,0:T(8,128)S(1)}, f32[32,32]{1,0:T(8,128)S(1)}, f32[32,32]{1,0:T(8,128)S(1)}, s32[]{:T(128)}, /*index=5*/s32[]{:T(128)}, ...), condition=%wide.region_4.0_spmd, body=%wide.region_3.0_spmd.sunk | while | flops 12419 | bytes 19449 | solution.py:19
  112.8 0.8 fusion.26
  114.2 0.8 fusion.26
  115.6 0.8 fusion.26
  117.0 0.8 fusion.26
  118.4 0.8 fusion.26
  119.8 0.8 fusion.26
  121.2 0.8 fusion.26
  122.6 0.8 fusion.26
  124.0 0.8 fusion.26
  126.9 0.8 fusion.26
  128.3 0.8 fusion.26
  129.7 0.8 fusion.26
  131.1 0.8 fusion.26
  157.3 12.2 %fusion.5 = f32[32,1,2048]{2,1,0:T(1,128)S(1)} fusion(f32[32,32,1]{1,2,0:T(1,128)S(1)} %bitcast.33, f32[32,32,2048]{2,0,1:T(8,128)} %fusion.10), kind=kOutput, calls=%fused_computation.8 | convolution fusion | flops 25165824 | bytes 8654848 | tf_op jit(solution)/shard_map/rij,ri->rj/dot_general | solution.py:43
  169.5 0.8 copy.18
  170.3 87.4 %all-reduce.2.cloned.1.call-done = f32[32,2048]{1,0:T(8,128)} async-done(((f32[32,2048]{1,0:T(8,128)}), f32[32,2048]{1,0:T(8,128)}) %all-reduce.2.cloned.1.call-update) | async-done | bytes 262160 | tf_op jit(solution)/shard_map/psum | solution.py:44
  257.7 1.5 dynamic-slice_multiply_fusion
  (93 shorter events, 34.7 us)
Async XLA Ops:
  7.2 31.2 %copy-start = (bf16[32,2048]{1,0:T(8,128)(2,1)S(1)}, bf16[32,2048]{1,0:T(8,128)(2,1)}, u32[]{:S(2)}) copy-start(bf16[32,2048]{1,0:T(8,128)(2,1)} %param.8) | copy-start | bytes 393220
  7.2 250.5 %all-reduce.2.cloned.1.call-start = ((), (), s32[]{:S(2)}) async-start(), calls=%async_computation | async-start | bytes 524288 | tf_op jit(solution)/shard_map/psum | solution.py:44
  38.4 73.8 %copy-start.2 = (f32[32,32]{1,0:T(8,128)S(1)}, f32[32,32]{1,0:T(8,128)}, u32[]{:S(2)}) copy-start(f32[32,32]{1,0:T(8,128)} %param.7) | copy-start | bytes 12292
  157.3 101.8 %copy-start.1 = (f32[32,32]{1,0:T(8,128)}, f32[32,32]{1,0:T(8,128)S(1)}, u32[]{:S(2)}) copy-start(f32[32,32]{1,0:T(8,128)S(1)} %get-tuple-element.124) | copy-start | bytes 12292
Sparse Core Ops, SparseCore 0:
  170.4 87.2 all-reduce.1
where the time goes:
time: 267 us; the launch traced here: 266 us
  waiting for transfers between devices  87.4 us (33%)
  matrix products  80.2 us (30%)
  blocking collectives  61.9 us (23%)
  local copies, waits for them, and re-layouts  20.5 us (8%)
  between operations  14.1 us (5%)
    psum x1, waiting for transfers between devices, local(): whole = lax.psum(term, ('roll', 'cross'))  87.4 us
    psum x1, blocking collectives, local(): mttkrp = lax.psum(local_terms, ('mach', 'cross'))  39.1 us
    dot_general x1, matrix products, local(): lax.dot_general(cross_factor, flat, (((1,), (1,)), ((), ())), preferred_e...  30.2 us
    dot_general x32, matrix products, column_step(): mixed = jnp.dot(gram_row, rows, precision=lax.Precision.HIGHEST)  25 us
    dynamic_slice x32, local copies, waits for them, and re-layouts, column_step(): diag_entry = lax.dynamic_slice_in_dim(gram_row, column, 1, 1)  18.8 us
    psum x1, blocking collectives, local(): gram_cross = lax.psum(local_cross, 'cross')  15.7 us
    dot_general x1, matrix products, local(): jnp.einsum('rij,ri->rj', partial_value, roll_factor, precision=lax.Precis...  12.2 us
    dot_general x1, matrix products, local(): jnp.einsum('rij,rj->ri', partial_value, mach_factor.astype(jnp.float32),...  11.7 us
  transfers between devices with their start and end apart: 1, of which 1 were waited for; matrix products, arithmetic and copies ran while one was open for 0% of the time, Pallas kernels for 0%

commit v1 on v0

v1 whole, which is shorter than its diff:
```python
import functools

import jax
import jax.numpy as jnp
from jax import lax
from jax.experimental import pallas as pl
from jax.experimental.pallas import tpu as pltpu
from jax.sharding import PartitionSpec as P

LANES = 128
MIB = 1024 * 1024


def stream_kernel(
    rolls_per_step, slots, density, mach_hbm, cross_hbm, partial, payload,
    block, mach, cross, weights, spread, terms, sem, factor_sem,
):
    rolls, bins, depth = density.shape
    rank = cross.shape[0]
    groups = LANES // rank
    span = bins // groups
    steps = rolls // rolls_per_step

    def fetch(step, slot):
        return pltpu.make_async_copy(
            density.at[pl.ds(step * rolls_per_step, rolls_per_step)], block.at[slot], sem.at[slot]
        )

    cross_fetch = pltpu.make_async_copy(cross_hbm, cross, factor_sem.at[0])
    mach_fetch = pltpu.make_async_copy(mach_hbm, mach, factor_sem.at[1])
    cross_fetch.start()
    mach_fetch.start()
    for slot in range(slots):
        fetch(slot, slot).start()

    cross_fetch.wait()
    cross_wide = cross[...].astype(jnp.float32)
    cross_lanes = jnp.concatenate([cross_wide] * groups, axis=0).T
    lane_group = lax.broadcasted_iota(jnp.int32, (depth, LANES), 1) // rank
    for group in range(groups):
        weights[group] = jnp.where(lane_group == group, cross_lanes, 0.0).astype(jnp.bfloat16)
    mach_fetch.wait()
    mach_wide = mach[...].astype(jnp.float32)
    spread[...] = jnp.concatenate(
        [mach_wide[:, group * span : (group + 1) * span] for group in range(groups)], axis=0
    ).T

    def one_step(step, carry):
        slot = lax.rem(step, slots)
        fetch(step, slot).wait()
        for part in range(rolls_per_step):
            value = jnp.dot(block[slot, part, 0:span, :], weights[0], preferred_element_type=jnp.float32)
            for group in range(1, groups):
                value = value + jnp.dot(
                    block[slot, part, group * span : (group + 1) * span, :],
                    weights[group],
                    preferred_element_type=jnp.float32,
                )
            roll = step * rolls_per_step + part
            partial[roll] = value
            terms[pl.ds(roll, 1), :] = jnp.sum(value * spread[...], axis=0, keepdims=True)

        @pl.when(step + slots < steps)
        def _():
            fetch(step + slots, slot).start()

        return carry

    lax.fori_loop(0, steps, one_step, 0)

    contract = (((1,), (1,)), ((), ()))
    gram_mach = lax.dot_general(mach[...], mach[...], contract, preferred_element_type=jnp.float32)
    gram_cross = lax.dot_general(cross[...], cross[...], contract, preferred_element_type=jnp.float32)
    summed = terms[:, 0:rank]
    for group in range(1, groups):
        summed = summed + terms[:, group * rank : (group + 1) * rank]
    filler = jnp.zeros((rank, LANES - 3 * rank), jnp.float32)
    payload[...] = jnp.concatenate([summed, gram_mach, gram_cross, filler], axis=1)


def stream(density, mach, cross):
    rolls, bins, depth = density.shape
    rank = cross.shape[0]
    groups = LANES // rank
    span = bins // groups
    rolls_per_step, slots = 2, 4
    in_hbm = functools.partial(pltpu.with_memory_space_constraint, memory_space=pltpu.HBM)
    anywhere = pl.BlockSpec(memory_space=pl.ANY)
    vmem = pl.BlockSpec(memory_space=pltpu.VMEM)
    return pl.pallas_call(
        functools.partial(stream_kernel, rolls_per_step, slots),
        out_shape=(
            pltpu.VMEM((rolls, span, LANES), jnp.float32),
            pltpu.VMEM((rolls, LANES), jnp.float32),
        ),
        in_specs=[anywhere, anywhere, anywhere],
        out_specs=(vmem, vmem),
        scratch_shapes=[
            pltpu.VMEM((slots, rolls_per_step, bins, depth), jnp.bfloat16),
            pltpu.VMEM(mach.shape, mach.dtype),
            pltpu.VMEM(cross.shape, cross.dtype),
            pltpu.VMEM((groups, depth, LANES), jnp.bfloat16),
            pltpu.VMEM((span, LANES), jnp.float32),
            pltpu.VMEM((rolls, LANES), jnp.float32),
            pltpu.SemaphoreType.DMA((slots,)),
            pltpu.SemaphoreType.DMA((2,)),
        ],
        compiler_params=pltpu.CompilerParams(vmem_limit_bytes=40 * MIB),
        cost_estimate=pl.CostEstimate(
            flops=2 * rolls * bins * depth * rank, bytes_accessed=2 * rolls * bins * depth, transcendentals=0
        ),
        name="stream",
    )(density, in_hbm(mach), in_hbm(cross))


def update_kernel(scale, place, partial, payload, start, roll_out, keep, send, total, roll_rows, sem):
    rolls, span, lanes = partial.shape
    rank = start.shape[0]
    groups = lanes // rank
    half = rank // 2
    flipped = payload[...].T
    gram = flipped[rank : 2 * rank] * flipped[2 * rank : 3 * rank]
    row_id = lax.broadcasted_iota(jnp.int32, (rank, rank), 0)
    lane_id = lax.broadcasted_iota(jnp.int32, (rank, rank), 1)
    diag = jnp.sum(jnp.where(row_id == lane_id, gram, 0.0), axis=1, keepdims=True)
    share = gram / diag
    rows = start[...]
    gap = flipped[0:rank] / diag
    for r in range(rank):
        gap = gap - share[:, r : r + 1] * rows[r : r + 1, :]
    done = []
    for r in range(rank):
        current = rows[r : r + 1, :]
        updated = jnp.maximum(current + gap[r : r + 1, :], 0.0)
        gap = gap - share[:, r : r + 1] * (updated - current)
        done.append(updated)
    factor = jnp.concatenate(done, axis=0)
    roll_rows[...] = factor
    store = pltpu.make_async_copy(roll_rows, roll_out, sem)
    store.start()
    factor_lanes = jnp.concatenate([factor * scale] * groups, axis=0).T

    chunk = min(span, 64)
    for first in range(0, span, chunk):
        value = partial[0, first : first + chunk, :] * factor_lanes[0:1, :]
        for roll in range(1, rolls):
            value = value + partial[roll, first : first + chunk, :] * factor_lanes[roll : roll + 1, :]
        total[first : first + chunk, :] = value
    blocks = total[...].T.reshape(groups, 2, half, span)
    core = place[0]
    cross_at = place[1]
    low_first = (0, 2, 1, 3)
    for slot, distance in enumerate(low_first):
        for group in range(groups):

            @pl.when(cross_at ^ distance == group)
            def _():
                @pl.when(core == 0)
                def _():
                    keep[slot] = blocks[group, 0]
                    send[slot] = blocks[group, 1]

                @pl.when(core != 0)
                def _():
                    keep[slot] = blocks[group, 1]
                    send[slot] = blocks[group, 0]

    store.wait()


def update(scale, place, partial, payload, start):
    rolls, span, lanes = partial.shape
    rank = start.shape[0]
    groups = lanes // rank
    vmem = pl.BlockSpec(memory_space=pltpu.VMEM)
    part = pltpu.VMEM((groups, rank // 2, span), jnp.float32)
    return pl.pallas_call(
        functools.partial(update_kernel, scale),
        out_shape=(jax.ShapeDtypeStruct((rank, rolls), jnp.float32), part, part),
        in_specs=[pl.BlockSpec(memory_space=pltpu.SMEM), vmem, vmem, vmem],
        out_specs=(pl.BlockSpec(memory_space=pl.ANY), vmem, vmem),
        scratch_shapes=[
            pltpu.VMEM((span, lanes), jnp.float32),
            pltpu.VMEM((rank, rolls), jnp.float32),
            pltpu.SemaphoreType.DMA,
        ],
        compiler_params=pltpu.CompilerParams(vmem_limit_bytes=40 * MIB),
        cost_estimate=pl.CostEstimate(flops=4 * rolls * span * lanes, bytes_accessed=0, transcendentals=0),
        name="update",
    )(place, pltpu.with_memory_space_constraint(partial, pltpu.VMEM), payload, start)


def swap(value, axes, distance):
    axes = axes if isinstance(axes, tuple) else (axes,)
    count = 1
    for axis in axes:
        count *= lax.axis_size(axis)
    return lax.ppermute(value, axes, [(source, source ^ distance) for source in range(count)])


def reduce_payload(payload, rank):
    mach_size, cross_size = lax.axis_size("mach"), lax.axis_size("cross")
    lane = lax.broadcasted_iota(jnp.int32, payload.shape, 1)
    is_term = lane < rank
    is_mach = jnp.logical_and(lane >= rank, lane < 2 * rank)
    is_cross = jnp.logical_and(lane >= 2 * rank, lane < 3 * rank)

    both = ("mach", "cross")
    over_mach = swap(payload, both, cross_size)
    over_cross = swap(payload, both, 1)
    over_both = swap(payload, both, cross_size + 1)
    payload = payload + (
        jnp.where(jnp.logical_or(is_term, is_mach), over_mach, 0.0)
        + jnp.where(jnp.logical_or(is_term, is_cross), over_cross, 0.0)
        + jnp.where(is_term, over_both, 0.0)
    )
    distance = 2
    while distance < mach_size:
        arrived = swap(payload, "mach", distance)
        payload = payload + jnp.where(is_cross, 0.0, arrived)
        distance *= 2
    distance = 2
    while distance < cross_size:
        arrived = swap(payload, "cross", distance)
        payload = payload + jnp.where(is_mach, 0.0, arrived)
        distance *= 2
    return payload


def reduce_blocks(keep, send):
    cross_size = lax.axis_size("cross")
    value = keep + swap(send, "roll", 1)
    mine, his = value[:2], value[2:]
    by_cross = swap(his, "cross", 1)
    by_roll = swap(mine, "roll", 2)
    by_both = swap(his, ("roll", "cross"), 2 * cross_size + 1)
    value = mine + (by_cross + (by_roll + by_both))
    value = value[0] + swap(value[1], "cross", 2)
    other = swap(value, "roll", 1)
    core = lax.axis_index("roll") % 2
    return jnp.where(
        core == 0, jnp.concatenate([value, other], axis=0), jnp.concatenate([other, value], axis=0)
    )


def local(density, roll_start, mach_factor, cross_factor):
    rolls_here, _, cross_here = density.shape
    rank = cross_factor.shape[0]
    all_rolls = rolls_here * lax.axis_size("roll")
    all_cross = cross_here * lax.axis_size("cross")
    scale = rank / (all_rolls * all_cross)
    place = jnp.stack([lax.axis_index("roll") % 2, lax.axis_index("cross")]).astype(jnp.int32)
    partial_value, payload = stream(density, mach_factor, cross_factor)
    payload = reduce_payload(payload, rank)
    roll_factor, keep, send = update(scale, place, partial_value, payload, roll_start)
    return (roll_factor, reduce_blocks(keep, send))


def solution(mesh):
    assert mesh.shape["roll"] == 4 and mesh.shape["cross"] == 4
    in_specs = (P("roll", "mach", "cross"), P(None, "roll"), P(None, "mach"), P(None, "cross"))
    out_specs = (P(None, "roll"), P(None, ("mach", "cross")))
    return jax.shard_map(local, mesh=mesh, in_specs=in_specs, out_specs=out_specs, check_vma=False)
```

time: 267 us -> 62.9 us (0.24)
  matrix products: 80.2 us -> 0 us
  waiting for transfers between devices: 87.4 us -> 14.1 us
  blocking collectives: 61.9 us -> 0 us
  Pallas kernels: 0 us -> 27 us
  local copies, waits for them, and re-layouts: 20.5 us -> 6.62 us
  starting transfers between devices: 0.04 us -> 13.5 us
  between operations: 14.1 us -> 0.75 us
    psum x1 -> x0, waiting for transfers between devices: 87.4 us -> none  [local(): whole = lax.psum(term, ('roll', 'cross'))]
    dot_general x37 -> x0, matrix products: 80.2 us -> none  [the longest x1 30.2 us: local(): lax.dot_general(cross_factor, flat, (((1,), (1,)), ((), ())), preferred_e...]
    psum x3 -> x0, blocking collectives: 61.9 us -> none  [the longest x1 39.1 us: local(): mttkrp = lax.psum(local_terms, ('mach', 'cross'))]
    pallas_call x0 -> x2, Pallas kernels: none -> 27 us  [the longest x1 25.1 us: stream(): pl.pallas_call(functools.partial(stream_kernel, rolls_per_step, slots), o...]
    dynamic_slice x32 -> x0, local copies, waits for them, and re-layouts: 18.8 us -> none  [column_step(): diag_entry = lax.dynamic_slice_in_dim(gram_row, column, 1, 1)]
    ppermute x0 -> x10, waiting for transfers between devices: none -> 14.1 us  [swap(): lax.ppermute(value, axes, [(source, source ^ distance) for source in rang...]
    ppermute x0 -> x10, starting transfers between devices: none -> 13.5 us  [swap(): lax.ppermute(value, axes, [(source, source ^ distance) for source in rang...]
    unnamed x6, local copies, waits for them, and re-layouts: 0.02 us -> 6.6 us
  transfers between devices with their start and end apart: 1 -> 10, of which waited for: 1 -> 10; matrix products, arithmetic and copies ran while one was open for 0% -> 0% of each run, Pallas kernels for 0% -> 0%
where the time goes in v1:
time: 62.9 us; the launch traced here: 62.7 us
  Pallas kernels  27 us (43%)
  waiting for transfers between devices  14.1 us (22%)
  starting transfers between devices  13.5 us (21%)
  local copies, waits for them, and re-layouts  6.62 us (11%)
  other arithmetic  0.79 us (1%)
  between operations  0.75 us (1%)
    pallas_call x1, Pallas kernels, stream(): pl.pallas_call(functools.partial(stream_kernel, rolls_per_step, slots), o...  25.1 us
    ppermute x10, waiting for transfers between devices, swap(): lax.ppermute(value, axes, [(source, source ^ distance) for source in rang...  14.1 us
    ppermute x10, starting transfers between devices, swap(): lax.ppermute(value, axes, [(source, source ^ distance) for source in rang...  13.5 us
    unnamed x6, local copies, waits for them, and re-layouts  6.6 us
    pallas_call x1, Pallas kernels, update(): pl.pallas_call(functools.partial(update_kernel, scale), out_shape=(jax.Sh...  1.91 us
  transfers between devices with their start and end apart: 10, of which 10 were waited for; matrix products, arithmetic and copies ran while one was open for 0% of the time, Pallas kernels for 0%

profile of v1, /device:TPU:0, one launch (start us, length us, event | category | flops | bytes accessed | tf_op | source)
XLA Modules:
  0.0 62.7 jit_solution(14044737017622376752)
XLA Ops:
  0.6 25.1 %stream.1 = (f32[32,512,128]{2,1,0:T(8,128)S(1)}, f32[32,128]{1,0:T(8,128)S(1)}) custom-call(bf16[32,2048,512]{2,1,0:T(8,128)(2,1)} %density.1, bf16[32,2048]{1,0:T(8,128)(2,1)} %mach_hbm.1, bf16[32,512]{1,0:T(8,128)(2,1)} %cross_hbm.1), custom_call_target="tpu_custom_call" | custom-call | flops 2147483648 | bytes 67108864 | tf_op jit(solution)/shard_map/stream/pallas_call | solution.py:90
  25.7 3.2 %copy-done = f32[32,512,128]{2,1,0:T(8,128)} copy-done((f32[32,512,128]{2,1,0:T(8,128)}, f32[32,512,128]{2,1,0:T(8,128)S(1)}, u32[]{:S(2)}) %copy-start) | copy-done | bytes 8388632
  28.9 4.0 %collective-permute-start.2 = (f32[32,128]{1,0:T(8,128)S(1)}, f32[32,128]{1,0:T(8,128)S(1)}, u32[]{:S(2)}, u32[]{:S(2)}) collective-permute-start(f32[32,128]{1,0:T(8,128)S(1)} %get-tuple-element.8), channel_id=1, source_target_pairs={{0,5},{1,4},{2,7},{3,6},{4,1},{5,0},{6,3},{7,2},{8,13},{9,12},{10,... | collective-permute-start | bytes 49160 | tf_op jit(solution)/shard_map/ppermute | solution.py:198
  32.9 0.4 collective-permute-start.1
  33.4 0.1 collective-permute-start
  33.5 1.1 %collective-permute-done.2 = f32[32,128]{1,0:T(8,128)S(1)} collective-permute-done((f32[32,128]{1,0:T(8,128)S(1)}, f32[32,128]{1,0:T(8,128)S(1)}, u32[]{:S(2)}, u32[]{:S(2)}) %collective-permute-start.2) | collective-permute-done | bytes 16416 | tf_op jit(solution)/shard_map/ppermute | solution.py:198
  34.6 2.0 %collective-permute-done.1 = f32[32,128]{1,0:T(8,128)S(1)} collective-permute-done((f32[32,128]{1,0:T(8,128)S(1)}, f32[32,128]{1,0:T(8,128)S(1)}, u32[]{:S(2)}, u32[]{:S(2)}) %collective-permute-start.1) | collective-permute-done | bytes 16416 | tf_op jit(solution)/shard_map/ppermute | solution.py:198
  36.7 0.4 collective-permute-done
  37.1 2.7 %collective-permute-start.3 = (f32[32,128]{1,0:T(8,128)S(1)}, f32[32,128]{1,0:T(8,128)S(1)}, u32[]{:S(2)}, u32[]{:S(2)}) collective-permute-start(f32[32,128]{1,0:T(8,128)S(1)} %add_add_fusion.1), channel_id=1, source_target_pairs={{0,2},{1,3},{2,0},{3,1},{4,6},{5,7},{6,4},{7,5},{8,10},{9,11},{10,... | collective-permute-start | bytes 49160 | tf_op jit(solution)/shard_map/ppermute | solution.py:198
  39.8 0.1 pad_add_fusion.place
  39.9 2.0 %collective-permute-done.3 = f32[32,128]{1,0:T(8,128)S(1)} collective-permute-done((f32[32,128]{1,0:T(8,128)S(1)}, f32[32,128]{1,0:T(8,128)S(1)}, u32[]{:S(2)}, u32[]{:S(2)}) %collective-permute-start.3) | collective-permute-done | bytes 16416 | tf_op jit(solution)/shard_map/ppermute | solution.py:198
  41.8 3.4 %copy-done.1 = f32[32,512,128]{2,1,0:T(8,128)S(1)} copy-done((f32[32,512,128]{2,1,0:T(8,128)S(1)}, f32[32,512,128]{2,1,0:T(8,128)}, u32[]{:S(2)}) %copy-start.1) | copy-done | bytes 8388632
  45.2 1.9 %update.1 = (f32[32,32]{1,0:T(8,128)}, f32[4,16,512]{2,1,0:T(8,128)S(1)}, f32[4,16,512]{2,1,0:T(8,128)S(1)}) custom-call(s32[2]{0:T(128)S(1)} %pad_add_fusion.place, f32[32,512,128]{2,1,0:T(8,128)S(1)} %copy-done.1, f32[32,128]{1,0:T(8,128)S(1)} %select_add_fusion.payload, f32[32,32]{1,0:T(8,128)S(1)} %copy-done.2), custom_call_target="tpu_custom_call" | custom-call | flops 8388608 | tf_op jit(solution)/shard_map/update/pallas_call | solution.py:177
  47.2 1.3 %collective-permute-done.4 = f32[4,16,512]{2,1,0:T(8,128)S(1)} collective-permute-done((f32[4,16,512]{2,1,0:T(8,128)S(1)}, f32[4,16,512]{2,1,0:T(8,128)S(1)}, u32[]{:S(2)}, u32[]{:S(2)}) %collective-permute-start.4) | collective-permute-done | bytes 131104 | tf_op jit(solution)/shard_map/ppermute | solution.py:198
  48.6 1.6 %collective-permute-start.6 = (f32[2,16,512]{2,1,0:T(8,128)S(1)}, f32[2,16,512]{2,1,0:T(8,128)S(1)}, u32[]{:S(2)}, u32[]{:S(2)}) collective-permute-start(f32[2,16,512]{2,1,0:T(8,128)S(1)} %get-tuple-element.12), channel_id=1, source_target_pairs={{0,16},{8,24},{16,0},{24,8},{1,17},{9,25},{17,1},{25,9},{2,18},{10... | collective-permute-start | bytes 196616 | tf_op jit(solution)/shard_map/ppermute | solution.py:198
  50.1 1.5 %collective-permute-start.7 = (f32[2,16,512]{2,1,0:T(8,128)S(1)}, f32[2,16,512]{2,1,0:T(8,128)S(1)}, u32[]{:S(2)}, u32[]{:S(2)}) collective-permute-start(f32[2,16,512]{2,1,0:T(8,128)S(1)} %get-tuple-element.13), channel_id=1, source_target_pairs={{0,17},{1,16},{2,19},{3,18},{8,25},{9,24},{10,27},{11,26},{16,1},{... | collective-permute-start | bytes 196616 | tf_op jit(solution)/shard_map/ppermute | solution.py:198
  51.7 0.5 collective-permute-start.5
  52.1 0.8 %collective-permute-done.6 = f32[2,16,512]{2,1,0:T(8,128)S(1)} collective-permute-done((f32[2,16,512]{2,1,0:T(8,128)S(1)}, f32[2,16,512]{2,1,0:T(8,128)S(1)}, u32[]{:S(2)}, u32[]{:S(2)}) %collective-permute-start.6) | collective-permute-done | bytes 65568 | tf_op jit(solution)/shard_map/ppermute | solution.py:198
  52.9 2.9 %collective-permute-done.7 = f32[2,16,512]{2,1,0:T(8,128)S(1)} collective-permute-done((f32[2,16,512]{2,1,0:T(8,128)S(1)}, f32[2,16,512]{2,1,0:T(8,128)S(1)}, u32[]{:S(2)}, u32[]{:S(2)}) %collective-permute-start.7) | collective-permute-done | bytes 65568 | tf_op jit(solution)/shard_map/ppermute | solution.py:198
  55.8 0.1 collective-permute-done.5
  56.0 2.7 %collective-permute-start.8 = (f32[16,512]{1,0:T(8,128)S(1)}, f32[16,512]{1,0:T(8,128)S(1)}, u32[]{:S(2)}, u32[]{:S(2)}) collective-permute-start(f32[16,512]{1,0:T(8,128)S(1)} %slice_bitcast_fusion), channel_id=1, source_target_pairs={{0,2},{1,3},{2,0},{3,1},{4,6},{5,7},{6,4},{7,5},{8,10},{9,11},{10,... | collective-permute-start | bytes 98312 | tf_op jit(solution)/shard_map/ppermute | solution.py:198
  58.7 2.2 %collective-permute-done.8 = f32[16,512]{1,0:T(8,128)S(1)} collective-permute-done((f32[16,512]{1,0:T(8,128)S(1)}, f32[16,512]{1,0:T(8,128)S(1)}, u32[]{:S(2)}, u32[]{:S(2)}) %collective-permute-start.8) | collective-permute-done | bytes 32800 | tf_op jit(solution)/shard_map/ppermute | solution.py:198
  60.9 1.2 %collective-permute-done.9 = f32[16,512]{1,0:T(8,128)S(1)} collective-permute-done((f32[16,512]{1,0:T(8,128)S(1)}, f32[16,512]{1,0:T(8,128)S(1)}, u32[]{:S(2)}, u32[]{:S(2)}) %collective-permute-start.9) | collective-permute-done | bytes 32800 | tf_op jit(solution)/shard_map/ppermute | solution.py:198
  62.1 0.6 %maximum_select_fusion = f32[32,512]{1,0:T(8,128)} fusion(f32[16,512]{1,0:T(8,128)S(1)} %collective-permute-done.9, f32[16,512]{1,0:T(8,128)S(1)} %fusion, pred[]{:T(512)S(6)} %eq.6), kind=kLoop, calls=%fused_computation | loop fusion | flops 49152 | bytes 131073 | tf_op jit(solution)/shard_map/jit(_where)/select_n | solution.py:241
  (16 shorter events, 0.2 us)
Async XLA Ops:
  0.6 41.2 %copy-start.2 = (f32[32,32]{1,0:T(8,128)S(1)}, f32[32,32]{1,0:T(8,128)}, u32[]{:S(2)}) copy-start(f32[32,32]{1,0:T(8,128)} %start.1) | copy-start | bytes 12292
  25.7 3.2 %copy-start = (f32[32,512,128]{2,1,0:T(8,128)}, f32[32,512,128]{2,1,0:T(8,128)S(1)}, u32[]{:S(2)}) copy-start(f32[32,512,128]{2,1,0:T(8,128)S(1)} %get-tuple-element.7.partial) | copy-start | bytes 25165828
  28.9 5.7 %collective-permute-start.2 = (f32[32,128]{1,0:T(8,128)S(1)}, f32[32,128]{1,0:T(8,128)S(1)}, u32[]{:S(2)}, u32[]{:S(2)}) collective-permute-start(f32[32,128]{1,0:T(8,128)S(1)} %get-tuple-element.8), channel_id=1, source_target_pairs={{0,5},{1,4},{2,7},{3,6},{4,1},{5,0},{6,3},{7,2},{8,13},{9,12},{10,... | collective-permute-start | bytes 49160 | tf_op jit(solution)/shard_map/ppermute | solution.py:198
  32.9 3.7 %collective-permute-start.1 = (f32[32,128]{1,0:T(8,128)S(1)}, f32[32,128]{1,0:T(8,128)S(1)}, u32[]{:S(2)}, u32[]{:S(2)}) collective-permute-start(f32[32,128]{1,0:T(8,128)S(1)} %get-tuple-element.8), channel_id=1, source_target_pairs={{0,1},{1,0},{2,3},{3,2},{4,5},{5,4},{6,7},{7,6},{8,9},{9,8},{10,11... | collective-permute-start | bytes 49160 | tf_op jit(solution)/shard_map/ppermute | solution.py:198
  33.4 3.7 %collective-permute-start = (f32[32,128]{1,0:T(8,128)S(1)}, f32[32,128]{1,0:T(8,128)S(1)}, u32[]{:S(2)}, u32[]{:S(2)}) collective-permute-start(f32[32,128]{1,0:T(8,128)S(1)} %get-tuple-element.8), channel_id=1, source_target_pairs={{0,4},{1,5},{2,6},{3,7},{4,0},{5,1},{6,2},{7,3},{8,12},{9,13},{10,... | collective-permute-start | bytes 49160 | tf_op jit(solution)/shard_map/ppermute | solution.py:198
  37.1 4.7 %collective-permute-start.3 = (f32[32,128]{1,0:T(8,128)S(1)}, f32[32,128]{1,0:T(8,128)S(1)}, u32[]{:S(2)}, u32[]{:S(2)}) collective-permute-start(f32[32,128]{1,0:T(8,128)S(1)} %add_add_fusion.1), channel_id=1, source_target_pairs={{0,2},{1,3},{2,0},{3,1},{4,6},{5,7},{6,4},{7,5},{8,10},{9,11},{10,... | collective-permute-start | bytes 49160 | tf_op jit(solution)/shard_map/ppermute | solution.py:198
  41.8 3.4 %copy-start.1 = (f32[32,512,128]{2,1,0:T(8,128)S(1)}, f32[32,512,128]{2,1,0:T(8,128)}, u32[]{:S(2)}) copy-start(f32[32,512,128]{2,1,0:T(8,128)} %copy-done) | copy-start | bytes 25165828
  47.1 1.4 %collective-permute-start.4 = (f32[4,16,512]{2,1,0:T(8,128)S(1)}, f32[4,16,512]{2,1,0:T(8,128)S(1)}, u32[]{:S(2)}, u32[]{:S(2)}) collective-permute-start(f32[4,16,512]{2,1,0:T(8,128)S(1)} %get-tuple-element.11), channel_id=1, source_target_pairs={{0,8},{8,0},{16,24},{24,16},{1,9},{9,1},{17,25},{25,17},{2,10},{10... | collective-permute-start | bytes 393224 | tf_op jit(solution)/shard_map/ppermute | solution.py:198
  48.6 4.3 %collective-permute-start.6 = (f32[2,16,512]{2,1,0:T(8,128)S(1)}, f32[2,16,512]{2,1,0:T(8,128)S(1)}, u32[]{:S(2)}, u32[]{:S(2)}) collective-permute-start(f32[2,16,512]{2,1,0:T(8,128)S(1)} %get-tuple-element.12), channel_id=1, source_target_pairs={{0,16},{8,24},{16,0},{24,8},{1,17},{9,25},{17,1},{25,9},{2,18},{10... | collective-permute-start | bytes 196616 | tf_op jit(solution)/shard_map/ppermute | solution.py:198
  50.1 5.7 %collective-permute-start.7 = (f32[2,16,512]{2,1,0:T(8,128)S(1)}, f32[2,16,512]{2,1,0:T(8,128)S(1)}, u32[]{:S(2)}, u32[]{:S(2)}) collective-permute-start(f32[2,16,512]{2,1,0:T(8,128)S(1)} %get-tuple-element.13), channel_id=1, source_target_pairs={{0,17},{1,16},{2,19},{3,18},{8,25},{9,24},{10,27},{11,26},{16,1},{... | collective-permute-start | bytes 196616 | tf_op jit(solution)/shard_map/ppermute | solution.py:198
  51.7 4.3 %collective-permute-start.5 = (f32[2,16,512]{2,1,0:T(8,128)S(1)}, f32[2,16,512]{2,1,0:T(8,128)S(1)}, u32[]{:S(2)}, u32[]{:S(2)}) collective-permute-start(f32[2,16,512]{2,1,0:T(8,128)S(1)} %get-tuple-element.13), channel_id=1, source_target_pairs={{0,1},{1,0},{2,3},{3,2},{4,5},{5,4},{6,7},{7,6},{8,9},{9,8},{10,11... | collective-permute-start | bytes 196616 | tf_op jit(solution)/shard_map/ppermute | solution.py:198
  56.0 4.9 %collective-permute-start.8 = (f32[16,512]{1,0:T(8,128)S(1)}, f32[16,512]{1,0:T(8,128)S(1)}, u32[]{:S(2)}, u32[]{:S(2)}) collective-permute-start(f32[16,512]{1,0:T(8,128)S(1)} %slice_bitcast_fusion), channel_id=1, source_target_pairs={{0,2},{1,3},{2,0},{3,1},{4,6},{5,7},{6,4},{7,5},{8,10},{9,11},{10,... | collective-permute-start | bytes 98312 | tf_op jit(solution)/shard_map/ppermute | solution.py:198
  60.9 1.2 %collective-permute-start.9 = (f32[16,512]{1,0:T(8,128)S(1)}, f32[16,512]{1,0:T(8,128)S(1)}, u32[]{:S(2)}, u32[]{:S(2)}) collective-permute-start(f32[16,512]{1,0:T(8,128)S(1)} %fusion), channel_id=1, source_target_pairs={{0,8},{8,0},{16,24},{24,16},{1,9},{9,1},{17,25},{25,17},{2,10},{10... | collective-permute-start | bytes 98312 | tf_op jit(solution)/shard_map/ppermute | solution.py:198

commit v2 on v1

--- a/solution.py
+++ b/solution.py
@@ -12,7 +12,7 @@
 
 
 def stream_kernel(
-    rolls_per_step, slots, density, mach_hbm, cross_hbm, partial, payload,
+    rolls_per_step, slots, ahead, density, mach_hbm, cross_hbm, partial, payload,
     block, mach, cross, weights, spread, terms, sem, factor_sem,
 ):
     rolls, bins, depth = density.shape
@@ -30,7 +30,7 @@
     mach_fetch = pltpu.make_async_copy(mach_hbm, mach, factor_sem.at[1])
     cross_fetch.start()
     mach_fetch.start()
-    for slot in range(slots):
+    for slot in range(ahead):
         fetch(slot, slot).start()
 
     cross_fetch.wait()
@@ -47,6 +47,11 @@
 
     def one_step(step, carry):
         slot = lax.rem(step, slots)
+
+        @pl.when(step + ahead < steps)
+        def _():
+            fetch(step + ahead, lax.rem(step + ahead, slots)).start()
+
         fetch(step, slot).wait()
         for part in range(rolls_per_step):
             value = jnp.dot(block[slot, part, 0:span, :], weights[0], preferred_element_type=jnp.float32)
@@ -59,11 +64,6 @@
             roll = step * rolls_per_step + part
             partial[roll] = value
             terms[pl.ds(roll, 1), :] = jnp.sum(value * spread[...], axis=0, keepdims=True)
-
-        @pl.when(step + slots < steps)
-        def _():
-            fetch(step + slots, slot).start()
-
         return carry
 
     lax.fori_loop(0, steps, one_step, 0)
@@ -83,12 +83,12 @@
     rank = cross.shape[0]
     groups = LANES // rank
     span = bins // groups
-    rolls_per_step, slots = 2, 4
+    rolls_per_step, slots, ahead = 2, 4, 2
     in_hbm = functools.partial(pltpu.with_memory_space_constraint, memory_space=pltpu.HBM)
     anywhere = pl.BlockSpec(memory_space=pl.ANY)
     vmem = pl.BlockSpec(memory_space=pltpu.VMEM)
     return pl.pallas_call(
-        functools.partial(stream_kernel, rolls_per_step, slots),
+        functools.partial(stream_kernel, rolls_per_step, slots, ahead),
         out_shape=(
             pltpu.VMEM((rolls, span, LANES), jnp.float32),
             pltpu.VMEM((rolls, LANES), jnp.float32),
@@ -113,7 +113,7 @@
     )(density, in_hbm(mach), in_hbm(cross))
 
 
-def update_kernel(scale, place, partial, payload, start, roll_out, keep, send, total, roll_rows, sem):
+def update_kernel(scale, partial, payload, start, roll_out, keep, send, total, blocks, roll_rows, sem):
     rolls, span, lanes = partial.shape
     rank = start.shape[0]
     groups = lanes // rank
@@ -146,29 +146,16 @@
         for roll in range(1, rolls):
             value = value + partial[roll, first : first + chunk, :] * factor_lanes[roll : roll + 1, :]
         total[first : first + chunk, :] = value
-    blocks = total[...].T.reshape(groups, 2, half, span)
-    core = place[0]
-    cross_at = place[1]
-    low_first = (0, 2, 1, 3)
-    for slot, distance in enumerate(low_first):
-        for group in range(groups):
-
-            @pl.when(cross_at ^ distance == group)
-            def _():
-                @pl.when(core == 0)
-                def _():
-                    keep[slot] = blocks[group, 0]
-                    send[slot] = blocks[group, 1]
-
-                @pl.when(core != 0)
-                def _():
-                    keep[slot] = blocks[group, 1]
-                    send[slot] = blocks[group, 0]
-
+    blocks[...] = total[...].T.reshape(groups, 2, half, span)
+    core = lax.rem(lax.axis_index("roll"), 2)
+    cross_at = lax.axis_index("cross")
+    for slot, distance in enumerate((0, 2, 1, 3)):
+        keep[slot] = blocks[cross_at ^ distance, core]
+        send[slot] = blocks[cross_at ^ distance, 1 - core]
     store.wait()
 
 
-def update(scale, place, partial, payload, start):
+def update(scale, partial, payload, start):
     rolls, span, lanes = partial.shape
     rank = start.shape[0]
     groups = lanes // rank
@@ -177,17 +164,18 @@
     return pl.pallas_call(
         functools.partial(update_kernel, scale),
         out_shape=(jax.ShapeDtypeStruct((rank, rolls), jnp.float32), part, part),
-        in_specs=[pl.BlockSpec(memory_space=pltpu.SMEM), vmem, vmem, vmem],
+        in_specs=[vmem, vmem, vmem],
         out_specs=(pl.BlockSpec(memory_space=pl.ANY), vmem, vmem),
         scratch_shapes=[
             pltpu.VMEM((span, lanes), jnp.float32),
+            pltpu.VMEM((groups, 2, rank // 2, span), jnp.float32),
             pltpu.VMEM((rank, rolls), jnp.float32),
             pltpu.SemaphoreType.DMA,
         ],
         compiler_params=pltpu.CompilerParams(vmem_limit_bytes=40 * MIB),
         cost_estimate=pl.CostEstimate(flops=4 * rolls * span * lanes, bytes_accessed=0, transcendentals=0),
         name="update",
-    )(place, pltpu.with_memory_space_constraint(partial, pltpu.VMEM), payload, start)
+    )(pltpu.with_memory_space_constraint(partial, pltpu.VMEM), payload, start)
 
 
 def swap(value, axes, distance):
@@ -236,11 +224,31 @@
     by_both = swap(his, ("roll", "cross"), 2 * cross_size + 1)
     value = mine + (by_cross + (by_roll + by_both))
     value = value[0] + swap(value[1], "cross", 2)
-    other = swap(value, "roll", 1)
-    core = lax.axis_index("roll") % 2
-    return jnp.where(
-        core == 0, jnp.concatenate([value, other], axis=0), jnp.concatenate([other, value], axis=0)
-    )
+    return join(value, swap(value, "roll", 1))
+
+
+def join_kernel(own, other, out, sem):
+    core = lax.rem(lax.axis_index("roll"), 2)
+    half = own.shape[0]
+    first = pltpu.make_async_copy(own, out.at[pl.ds(pl.multiple_of(core * half, half), half)], sem.at[0])
+    second = pltpu.make_async_copy(other, out.at[pl.ds(pl.multiple_of((1 - core) * half, half), half)], sem.at[1])
+    first.start()
+    second.start()
+    first.wait()
+    second.wait()
+
+
+def join(own, other):
+    vmem = pl.BlockSpec(memory_space=pltpu.VMEM)
+    return pl.pallas_call(
+        join_kernel,
+        out_shape=jax.ShapeDtypeStruct((2 * own.shape[0], own.shape[1]), own.dtype),
+        in_specs=[vmem, vmem],
+        out_specs=pl.BlockSpec(memory_space=pl.ANY),
+        scratch_shapes=[pltpu.SemaphoreType.DMA((2,))],
+        compiler_params=pltpu.CompilerParams(vmem_limit_bytes=8 * MIB),
+        name="join",
+    )(own, other)
 
 
 def local(density, roll_start, mach_factor, cross_factor):
@@ -249,10 +257,9 @@
     all_rolls = rolls_here * lax.axis_size("roll")
     all_cross = cross_here * lax.axis_size("cross")
     scale = rank / (all_rolls * all_cross)
-    place = jnp.stack([lax.axis_index("roll") % 2, lax.axis_index("cross")]).astype(jnp.int32)
     partial_value, payload = stream(density, mach_factor, cross_factor)
     payload = reduce_payload(payload, rank)
-    roll_factor, keep, send = update(scale, place, partial_value, payload, roll_start)
+    roll_factor, keep, send = update(scale, partial_value, payload, roll_start)
     return (roll_factor, reduce_blocks(keep, send))
 
 

time: 62.9 us -> 53.5 us (0.85)
  local copies, waits for them, and re-layouts: 6.62 us -> 0.02 us
  Pallas kernels: 27 us -> 24.8 us
  other arithmetic: 0.79 us -> 0.08 us
    unnamed x6 -> x2, local copies, waits for them, and re-layouts: 6.6 us -> 0.01 us
    pallas_call x1 -> x2, Pallas kernels: 25.1 us -> 23.5 us  [the longest x1 22.9 us: stream(): pl.pallas_call(functools.partial(stream_kernel, rolls_per_step, slots, ah...]
    select_n x1 -> x0, other arithmetic: 0.64 us -> none  [reduce_blocks(): jnp.where(core == 0, jnp.concatenate([value, other], axis=0), jnp.concate...]
where the time goes in v2:
time: 53.5 us; the launch traced here: 53.4 us
  Pallas kernels  24.8 us (46%)
  waiting for transfers between devices  14.1 us (26%)
  starting transfers between devices  13.7 us (26%)
  between operations  0.71 us (1%)
    pallas_call x1, Pallas kernels, stream(): pl.pallas_call(functools.partial(stream_kernel, rolls_per_step, slots, ah...  22.9 us
    ppermute x10, waiting for transfers between devices, swap(): lax.ppermute(value, axes, [(source, source ^ distance) for source in rang...  14.1 us
    ppermute x10, starting transfers between devices, swap(): lax.ppermute(value, axes, [(source, source ^ distance) for source in rang...  13.7 us
    pallas_call x1, Pallas kernels, update(): pl.pallas_call(functools.partial(update_kernel, scale), out_shape=(jax.Sh...  1.3 us
  transfers between devices with their start and end apart: 10, of which 10 were waited for; matrix products, arithmetic and copies ran while one was open for 0% of the time, Pallas kernels for 0%

profile of v2, /device:TPU:0, one launch (start us, length us, event | category | flops | bytes accessed | tf_op | source)
XLA Modules:
  0.0 53.4 jit_solution(278905573284188338)
XLA Ops:
  0.6 0.0 copy-start
  0.6 22.9 %stream.1 = (f32[32,512,128]{2,1,0:T(8,128)S(1)}, f32[32,128]{1,0:T(8,128)S(1)}) custom-call(bf16[32,2048,512]{2,1,0:T(8,128)(2,1)} %density.1, bf16[32,2048]{1,0:T(8,128)(2,1)} %mach_hbm.1, bf16[32,512]{1,0:T(8,128)(2,1)} %cross_hbm.1), custom_call_target="tpu_custom_call" | custom-call | flops 2147483648 | bytes 67108864 | tf_op jit(solution)/shard_map/stream/pallas_call | solution.py:90
  23.5 4.0 %collective-permute-start.2 = (f32[32,128]{1,0:T(8,128)S(1)}, f32[32,128]{1,0:T(8,128)S(1)}, u32[]{:S(2)}, u32[]{:S(2)}) collective-permute-start(f32[32,128]{1,0:T(8,128)S(1)} %get-tuple-element.8), channel_id=1, source_target_pairs={{0,5},{1,4},{2,7},{3,6},{4,1},{5,0},{6,3},{7,2},{8,13},{9,12},{10,... | collective-permute-start | bytes 49160 | tf_op jit(solution)/shard_map/ppermute | solution.py:186
  27.5 0.4 collective-permute-start.1
  28.0 0.2 collective-permute-start
  28.2 1.1 %collective-permute-done.2 = f32[32,128]{1,0:T(8,128)S(1)} collective-permute-done((f32[32,128]{1,0:T(8,128)S(1)}, f32[32,128]{1,0:T(8,128)S(1)}, u32[]{:S(2)}, u32[]{:S(2)}) %collective-permute-start.2) | collective-permute-done | bytes 16416 | tf_op jit(solution)/shard_map/ppermute | solution.py:186
  29.3 2.0 %collective-permute-done.1 = f32[32,128]{1,0:T(8,128)S(1)} collective-permute-done((f32[32,128]{1,0:T(8,128)S(1)}, f32[32,128]{1,0:T(8,128)S(1)}, u32[]{:S(2)}, u32[]{:S(2)}) %collective-permute-start.1) | collective-permute-done | bytes 16416 | tf_op jit(solution)/shard_map/ppermute | solution.py:186
  31.3 0.4 collective-permute-done
  31.7 2.7 %collective-permute-start.3 = (f32[32,128]{1,0:T(8,128)S(1)}, f32[32,128]{1,0:T(8,128)S(1)}, u32[]{:S(2)}, u32[]{:S(2)}) collective-permute-start(f32[32,128]{1,0:T(8,128)S(1)} %add_add_fusion.1), channel_id=1, source_target_pairs={{0,2},{1,3},{2,0},{3,1},{4,6},{5,7},{6,4},{7,5},{8,10},{9,11},{10,... | collective-permute-start | bytes 49160 | tf_op jit(solution)/shard_map/ppermute | solution.py:186
  34.4 2.0 %collective-permute-done.3 = f32[32,128]{1,0:T(8,128)S(1)} collective-permute-done((f32[32,128]{1,0:T(8,128)S(1)}, f32[32,128]{1,0:T(8,128)S(1)}, u32[]{:S(2)}, u32[]{:S(2)}) %collective-permute-start.3) | collective-permute-done | bytes 16416 | tf_op jit(solution)/shard_map/ppermute | solution.py:186
  36.5 1.3 %update.1 = (f32[32,32]{1,0:T(8,128)}, f32[4,16,512]{2,1,0:T(8,128)S(1)}, f32[4,16,512]{2,1,0:T(8,128)S(1)}) custom-call(f32[32,512,128]{2,1,0:T(8,128)S(1)} %get-tuple-element.7.partial, f32[32,128]{1,0:T(8,128)S(1)} %select_add_fusion.payload, f32[32,32]{1,0:T(8,128)S(1)} %copy-done), custom_call_target="tpu_custom_call" | custom-call | flops 8388608 | tf_op jit(solution)/shard_map/update/pallas_call | solution.py:164
  37.8 0.1 collective-permute-start.4
  37.8 1.3 %collective-permute-done.4 = f32[4,16,512]{2,1,0:T(8,128)S(1)} collective-permute-done((f32[4,16,512]{2,1,0:T(8,128)S(1)}, f32[4,16,512]{2,1,0:T(8,128)S(1)}, u32[]{:S(2)}, u32[]{:S(2)}) %collective-permute-start.4) | collective-permute-done | bytes 131104 | tf_op jit(solution)/shard_map/ppermute | solution.py:186
  39.2 1.6 %collective-permute-start.6 = (f32[2,16,512]{2,1,0:T(8,128)S(1)}, f32[2,16,512]{2,1,0:T(8,128)S(1)}, u32[]{:S(2)}, u32[]{:S(2)}) collective-permute-start(f32[2,16,512]{2,1,0:T(8,128)S(1)} %get-tuple-element.12), channel_id=1, source_target_pairs={{0,16},{8,24},{16,0},{24,8},{1,17},{9,25},{17,1},{25,9},{2,18},{10... | collective-permute-start | bytes 196616 | tf_op jit(solution)/shard_map/ppermute | solution.py:186
  40.8 1.6 %collective-permute-start.7 = (f32[2,16,512]{2,1,0:T(8,128)S(1)}, f32[2,16,512]{2,1,0:T(8,128)S(1)}, u32[]{:S(2)}, u32[]{:S(2)}) collective-permute-start(f32[2,16,512]{2,1,0:T(8,128)S(1)} %get-tuple-element.13), channel_id=1, source_target_pairs={{0,17},{1,16},{2,19},{3,18},{8,25},{9,24},{10,27},{11,26},{16,1},{... | collective-permute-start | bytes 196616 | tf_op jit(solution)/shard_map/ppermute | solution.py:186
  42.3 0.4 collective-permute-start.5
  42.8 0.8 %collective-permute-done.6 = f32[2,16,512]{2,1,0:T(8,128)S(1)} collective-permute-done((f32[2,16,512]{2,1,0:T(8,128)S(1)}, f32[2,16,512]{2,1,0:T(8,128)S(1)}, u32[]{:S(2)}, u32[]{:S(2)}) %collective-permute-start.6) | collective-permute-done | bytes 65568 | tf_op jit(solution)/shard_map/ppermute | solution.py:186
  43.6 2.9 %collective-permute-done.7 = f32[2,16,512]{2,1,0:T(8,128)S(1)} collective-permute-done((f32[2,16,512]{2,1,0:T(8,128)S(1)}, f32[2,16,512]{2,1,0:T(8,128)S(1)}, u32[]{:S(2)}, u32[]{:S(2)}) %collective-permute-start.7) | collective-permute-done | bytes 65568 | tf_op jit(solution)/shard_map/ppermute | solution.py:186
  46.4 0.1 collective-permute-done.5
  46.6 2.7 %collective-permute-start.8 = (f32[16,512]{1,0:T(8,128)S(1)}, f32[16,512]{1,0:T(8,128)S(1)}, u32[]{:S(2)}, u32[]{:S(2)}) collective-permute-start(f32[16,512]{1,0:T(8,128)S(1)} %slice_bitcast_fusion), channel_id=1, source_target_pairs={{0,2},{1,3},{2,0},{3,1},{4,6},{5,7},{6,4},{7,5},{8,10},{9,11},{10,... | collective-permute-start | bytes 98312 | tf_op jit(solution)/shard_map/ppermute | solution.py:186
  49.3 2.2 %collective-permute-done.8 = f32[16,512]{1,0:T(8,128)S(1)} collective-permute-done((f32[16,512]{1,0:T(8,128)S(1)}, f32[16,512]{1,0:T(8,128)S(1)}, u32[]{:S(2)}, u32[]{:S(2)}) %collective-permute-start.8) | collective-permute-done | bytes 32800 | tf_op jit(solution)/shard_map/ppermute | solution.py:186
  51.5 0.0 collective-permute-start.9
  51.5 1.2 %collective-permute-done.9.other = f32[16,512]{1,0:T(8,128)S(1)} collective-permute-done((f32[16,512]{1,0:T(8,128)S(1)}, f32[16,512]{1,0:T(8,128)S(1)}, u32[]{:S(2)}, u32[]{:S(2)}) %collective-permute-start.9) | collective-permute-done | bytes 32800 | tf_op jit(solution)/shard_map/ppermute | solution.py:186
  52.7 0.6 %join.1 = f32[32,512]{1,0:T(8,128)} custom-call(f32[16,512]{1,0:T(8,128)S(1)} %fusion.own, f32[16,512]{1,0:T(8,128)S(1)} %collective-permute-done.9.other), custom_call_target="tpu_custom_call" | custom-call | tf_op jit(solution)/shard_map/join/pallas_call | solution.py:243
  (11 shorter events, 0.1 us)
Async XLA Ops:
  0.6 35.8 %copy-start = (f32[32,32]{1,0:T(8,128)S(1)}, f32[32,32]{1,0:T(8,128)}, u32[]{:S(2)}) copy-start(f32[32,32]{1,0:T(8,128)} %start.1) | copy-start | bytes 12292
  23.5 5.8 %collective-permute-start.2 = (f32[32,128]{1,0:T(8,128)S(1)}, f32[32,128]{1,0:T(8,128)S(1)}, u32[]{:S(2)}, u32[]{:S(2)}) collective-permute-start(f32[32,128]{1,0:T(8,128)S(1)} %get-tuple-element.8), channel_id=1, source_target_pairs={{0,5},{1,4},{2,7},{3,6},{4,1},{5,0},{6,3},{7,2},{8,13},{9,12},{10,... | collective-permute-start | bytes 49160 | tf_op jit(solution)/shard_map/ppermute | solution.py:186
  27.5 3.7 %collective-permute-start.1 = (f32[32,128]{1,0:T(8,128)S(1)}, f32[32,128]{1,0:T(8,128)S(1)}, u32[]{:S(2)}, u32[]{:S(2)}) collective-permute-start(f32[32,128]{1,0:T(8,128)S(1)} %get-tuple-element.8), channel_id=1, source_target_pairs={{0,1},{1,0},{2,3},{3,2},{4,5},{5,4},{6,7},{7,6},{8,9},{9,8},{10,11... | collective-permute-start | bytes 49160 | tf_op jit(solution)/shard_map/ppermute | solution.py:186
  28.0 3.7 %collective-permute-start = (f32[32,128]{1,0:T(8,128)S(1)}, f32[32,128]{1,0:T(8,128)S(1)}, u32[]{:S(2)}, u32[]{:S(2)}) collective-permute-start(f32[32,128]{1,0:T(8,128)S(1)} %get-tuple-element.8), channel_id=1, source_target_pairs={{0,4},{1,5},{2,6},{3,7},{4,0},{5,1},{6,2},{7,3},{8,12},{9,13},{10,... | collective-permute-start | bytes 49160 | tf_op jit(solution)/shard_map/ppermute | solution.py:186
  31.7 4.7 %collective-permute-start.3 = (f32[32,128]{1,0:T(8,128)S(1)}, f32[32,128]{1,0:T(8,128)S(1)}, u32[]{:S(2)}, u32[]{:S(2)}) collective-permute-start(f32[32,128]{1,0:T(8,128)S(1)} %add_add_fusion.1), channel_id=1, source_target_pairs={{0,2},{1,3},{2,0},{3,1},{4,6},{5,7},{6,4},{7,5},{8,10},{9,11},{10,... | collective-permute-start | bytes 49160 | tf_op jit(solution)/shard_map/ppermute | solution.py:186
  37.8 1.4 %collective-permute-start.4 = (f32[4,16,512]{2,1,0:T(8,128)S(1)}, f32[4,16,512]{2,1,0:T(8,128)S(1)}, u32[]{:S(2)}, u32[]{:S(2)}) collective-permute-start(f32[4,16,512]{2,1,0:T(8,128)S(1)} %get-tuple-element.11), channel_id=1, source_target_pairs={{0,8},{8,0},{16,24},{24,16},{1,9},{9,1},{17,25},{25,17},{2,10},{10... | collective-permute-start | bytes 393224 | tf_op jit(solution)/shard_map/ppermute | solution.py:186
  39.2 4.3 %collective-permute-start.6 = (f32[2,16,512]{2,1,0:T(8,128)S(1)}, f32[2,16,512]{2,1,0:T(8,128)S(1)}, u32[]{:S(2)}, u32[]{:S(2)}) collective-permute-start(f32[2,16,512]{2,1,0:T(8,128)S(1)} %get-tuple-element.12), channel_id=1, source_target_pairs={{0,16},{8,24},{16,0},{24,8},{1,17},{9,25},{17,1},{25,9},{2,18},{10... | collective-permute-start | bytes 196616 | tf_op jit(solution)/shard_map/ppermute | solution.py:186
  40.8 5.7 %collective-permute-start.7 = (f32[2,16,512]{2,1,0:T(8,128)S(1)}, f32[2,16,512]{2,1,0:T(8,128)S(1)}, u32[]{:S(2)}, u32[]{:S(2)}) collective-permute-start(f32[2,16,512]{2,1,0:T(8,128)S(1)} %get-tuple-element.13), channel_id=1, source_target_pairs={{0,17},{1,16},{2,19},{3,18},{8,25},{9,24},{10,27},{11,26},{16,1},{... | collective-permute-start | bytes 196616 | tf_op jit(solution)/shard_map/ppermute | solution.py:186
  42.3 4.3 %collective-permute-start.5 = (f32[2,16,512]{2,1,0:T(8,128)S(1)}, f32[2,16,512]{2,1,0:T(8,128)S(1)}, u32[]{:S(2)}, u32[]{:S(2)}) collective-permute-start(f32[2,16,512]{2,1,0:T(8,128)S(1)} %get-tuple-element.13), channel_id=1, source_target_pairs={{0,1},{1,0},{2,3},{3,2},{4,5},{5,4},{6,7},{7,6},{8,9},{9,8},{10,11... | collective-permute-start | bytes 196616 | tf_op jit(solution)/shard_map/ppermute | solution.py:186
  46.6 4.9 %collective-permute-start.8 = (f32[16,512]{1,0:T(8,128)S(1)}, f32[16,512]{1,0:T(8,128)S(1)}, u32[]{:S(2)}, u32[]{:S(2)}) collective-permute-start(f32[16,512]{1,0:T(8,128)S(1)} %slice_bitcast_fusion), channel_id=1, source_target_pairs={{0,2},{1,3},{2,0},{3,1},{4,6},{5,7},{6,4},{7,5},{8,10},{9,11},{10,... | collective-permute-start | bytes 98312 | tf_op jit(solution)/shard_map/ppermute | solution.py:186
  51.5 1.2 %collective-permute-start.9 = (f32[16,512]{1,0:T(8,128)S(1)}, f32[16,512]{1,0:T(8,128)S(1)}, u32[]{:S(2)}, u32[]{:S(2)}) collective-permute-start(f32[16,512]{1,0:T(8,128)S(1)} %fusion.own), channel_id=1, source_target_pairs={{0,8},{8,0},{16,24},{24,16},{1,9},{9,1},{17,25},{25,17},{2,10},{10... | collective-permute-start | bytes 98312 | tf_op jit(solution)/shard_map/ppermute | solution.py:186

commit v3 on v2

--- a/solution.py
+++ b/solution.py
@@ -9,73 +9,138 @@
 
 LANES = 128
 MIB = 1024 * 1024
+WIDE = 256
+UNITS = 2
 
 
 def stream_kernel(
-    rolls_per_step, slots, ahead, density, mach_hbm, cross_hbm, partial, payload,
-    block, mach, cross, weights, spread, terms, sem, factor_sem,
+    density, mach_hbm, cross_hbm, partial, payload,
+    block, mach, cross, weights, spread, terms, mach_rows, cross_rows, grams, sem, factor_sem,
 ):
     rolls, bins, depth = density.shape
     rank = cross.shape[0]
     groups = LANES // rank
     span = bins // groups
-    steps = rolls // rolls_per_step
-
-    def fetch(step, slot):
-        return pltpu.make_async_copy(
-            density.at[pl.ds(step * rolls_per_step, rolls_per_step)], block.at[slot], sem.at[slot]
-        )
+    slots = block.shape[0]
+    ahead = 4
+    tiles = 2 * groups
+    tile_rows = span // 2
+    part_rows = min(tile_rows, 128)
+    parts = tile_rows // part_rows
+
+    def fetch(roll, slot):
+        return pltpu.make_async_copy(density.at[roll], block.at[slot], sem.at[slot])
 
     cross_fetch = pltpu.make_async_copy(cross_hbm, cross, factor_sem.at[0])
     mach_fetch = pltpu.make_async_copy(mach_hbm, mach, factor_sem.at[1])
     cross_fetch.start()
     mach_fetch.start()
-    for slot in range(ahead):
-        fetch(slot, slot).start()
-
-    cross_fetch.wait()
-    cross_wide = cross[...].astype(jnp.float32)
-    cross_lanes = jnp.concatenate([cross_wide] * groups, axis=0).T
-    lane_group = lax.broadcasted_iota(jnp.int32, (depth, LANES), 1) // rank
-    for group in range(groups):
-        weights[group] = jnp.where(lane_group == group, cross_lanes, 0.0).astype(jnp.bfloat16)
-    mach_fetch.wait()
-    mach_wide = mach[...].astype(jnp.float32)
-    spread[...] = jnp.concatenate(
-        [mach_wide[:, group * span : (group + 1) * span] for group in range(groups)], axis=0
-    ).T
-
-    def one_step(step, carry):
-        slot = lax.rem(step, slots)
-
-        @pl.when(step + ahead < steps)
-        def _():
-            fetch(step + ahead, lax.rem(step + ahead, slots)).start()
-
-        fetch(step, slot).wait()
-        for part in range(rolls_per_step):
-            value = jnp.dot(block[slot, part, 0:span, :], weights[0], preferred_element_type=jnp.float32)
-            for group in range(1, groups):
-                value = value + jnp.dot(
-                    block[slot, part, group * span : (group + 1) * span, :],
-                    weights[group],
-                    preferred_element_type=jnp.float32,
-                )
-            roll = step * rolls_per_step + part
-            partial[roll] = value
-            terms[pl.ds(roll, 1), :] = jnp.sum(value * spread[...], axis=0, keepdims=True)
-        return carry
-
-    lax.fori_loop(0, steps, one_step, 0)
-
-    contract = (((1,), (1,)), ((), ()))
-    gram_mach = lax.dot_general(mach[...], mach[...], contract, preferred_element_type=jnp.float32)
-    gram_cross = lax.dot_general(cross[...], cross[...], contract, preferred_element_type=jnp.float32)
+    fetch(0, 0).start()
+
+    def multiply(*sums):
+        turns, gram_sums = sums[:-UNITS], sums[-UNITS:]
+
+        def sum_of(turn, unit, part):
+            return turns[(turn * UNITS + unit) * parts + part]
+
+        def issue(turn, slot, tile):
+            for unit in range(UNITS):
+                pltpu.matmul_push_rhs(weights[tile, unit * WIDE : (unit + 1) * WIDE, :], tile % 2, unit)
+            for part in range(parts):
+                first = tile * tile_rows + part * part_rows
+                for unit in range(UNITS):
+                    pltpu.matmul_acc_lhs(
+                        sum_of(turn, unit, part),
+                        block[slot, first : first + part_rows, unit * WIDE : (unit + 1) * WIDE],
+                        load_staged_rhs=tile % 2 if part == 0 else None,
+                    )
+
+        def collect(turn, roll, part):
+            value = pltpu.matmul_pop(sum_of(turn, 0, part)) + pltpu.matmul_pop(sum_of(turn, 1, part))
+            total = None
+            for half in range(2):
+                first = half * tile_rows + part * part_rows
+                piece = value[:, half * LANES : (half + 1) * LANES]
+                partial[roll, first : first + part_rows, :] = piece
+                weighted = piece * spread[first : first + part_rows, :]
+                total = weighted if total is None else total + weighted
+            return jnp.sum(total, axis=0, keepdims=True)
+
+        def finish(roll, pieces):
+            terms[pl.ds(roll, 1), :] = sum(pieces[1:], pieces[0])
+
+        def one_roll(turn, slot, roll_before):
+            pieces = []
+            for tile in range(tiles):
+                issue(turn, slot, tile)
+                for part in range(tile * parts // tiles, (tile + 1) * parts // tiles):
+                    pieces.append(collect(1 - turn, roll_before, part))
+            finish(roll_before, pieces)
+
+        cross_fetch.wait()
+        fetch(1, 1).start()
+        fetch(2, 2).start()
+        cross_lanes = jnp.concatenate([cross[...].astype(jnp.float32)] * groups, axis=0).T
+        lane_group = lax.broadcasted_iota(jnp.int32, (depth, LANES), 1) // rank
+        blank = jnp.zeros((depth, LANES), jnp.bfloat16)
+        for tile in range(tiles):
+            near, far = tile % 2 * LANES, (1 - tile % 2) * LANES
+            placed = jnp.where(lane_group == tile // 2, cross_lanes, 0.0).astype(jnp.bfloat16)
+            weights[tile, :, near : near + LANES] = placed
+            weights[tile, :, far : far + LANES] = blank
+        mach_fetch.wait()
+        fetch(3, 3).start()
+        spread[...] = jnp.concatenate(
+            [mach[:, group * span : (group + 1) * span].astype(jnp.float32) for group in range(groups)], axis=0
+        ).T
+
+        for part in range(parts):
+            collect(0, 0, part)
+        for unit in range(UNITS):
+            pltpu.matmul_pop(gram_sums[unit])
+
+        mach_rows[...] = jnp.zeros_like(mach_rows)
+        mach_rows[rank : 2 * rank, :] = mach[...]
+        cross_rows[...] = jnp.zeros_like(cross_rows)
+        cross_rows[2 * rank : 3 * rank, :] = cross[...]
+        work = [(mach_rows, mach, first) for first in range(0, bins, WIDE)]
+        work += [(cross_rows, cross, first) for first in range(0, depth, WIDE)]
+        for count, (right, left, first) in enumerate(work):
+            unit, stage = count % UNITS, count // UNITS % 2
+            pltpu.matmul_push_rhs(right[:, first : first + WIDE], stage, unit, transpose=True)
+            pltpu.matmul_acc_lhs(gram_sums[unit], left[:, first : first + WIDE], load_staged_rhs=stage)
+        grams[...] = (pltpu.matmul_pop(gram_sums[0]) + pltpu.matmul_pop(gram_sums[1]))[:, 0:LANES]
+
+        def two_rolls(step, carry):
+            roll = 2 * step
+            slot = lax.rem(roll, slots)
+
+            @pl.when(roll + ahead < rolls)
+            def _():
+                next_slot = lax.rem(roll + ahead, slots)
+                fetch(roll + ahead, next_slot).start()
+                fetch(roll + ahead + 1, next_slot + 1).start()
+
+            fetch(roll, slot).wait()
+            one_roll(0, slot, jnp.maximum(roll - 1, 0))
+            fetch(roll + 1, slot + 1).wait()
+            one_roll(1, slot + 1, roll)
+            return carry
+
+        lax.fori_loop(0, rolls // 2, two_rolls, 0)
+        finish(rolls - 1, [collect(1, rolls - 1, part) for part in range(parts)])
+
+    pl.run_scoped(
+        multiply,
+        *[pltpu.ACC(unit)((part_rows, WIDE), jnp.float32) for _ in range(2) for unit in range(UNITS) for _ in range(parts)],
+        *[pltpu.ACC(unit)((rank, WIDE), jnp.float32) for unit in range(UNITS)],
+    )
+
     summed = terms[:, 0:rank]
     for group in range(1, groups):
         summed = summed + terms[:, group * rank : (group + 1) * rank]
-    filler = jnp.zeros((rank, LANES - 3 * rank), jnp.float32)
-    payload[...] = jnp.concatenate([summed, gram_mach, gram_cross, filler], axis=1)
+    payload[...] = grams[...]
+    payload[:, 0:rank] = summed
 
 
 def stream(density, mach, cross):
@@ -83,12 +148,13 @@
     rank = cross.shape[0]
     groups = LANES // rank
     span = bins // groups
-    rolls_per_step, slots, ahead = 2, 4, 2
+    slots = 8
+    assert rolls == rank and depth == UNITS * WIDE
     in_hbm = functools.partial(pltpu.with_memory_space_constraint, memory_space=pltpu.HBM)
     anywhere = pl.BlockSpec(memory_space=pl.ANY)
     vmem = pl.BlockSpec(memory_space=pltpu.VMEM)
     return pl.pallas_call(
-        functools.partial(stream_kernel, rolls_per_step, slots, ahead),
+        stream_kernel,
         out_shape=(
             pltpu.VMEM((rolls, span, LANES), jnp.float32),
             pltpu.VMEM((rolls, LANES), jnp.float32),
@@ -96,12 +162,15 @@
         in_specs=[anywhere, anywhere, anywhere],
         out_specs=(vmem, vmem),
         scratch_shapes=[
-            pltpu.VMEM((slots, rolls_per_step, bins, depth), jnp.bfloat16),
+            pltpu.VMEM((slots, bins, depth), jnp.bfloat16),
             pltpu.VMEM(mach.shape, mach.dtype),
             pltpu.VMEM(cross.shape, cross.dtype),
-            pltpu.VMEM((groups, depth, LANES), jnp.bfloat16),
+            pltpu.VMEM((2 * groups, depth, WIDE), jnp.bfloat16),
             pltpu.VMEM((span, LANES), jnp.float32),
             pltpu.VMEM((rolls, LANES), jnp.float32),
+            pltpu.VMEM((WIDE, bins), jnp.bfloat16),
+            pltpu.VMEM((WIDE, depth), jnp.bfloat16),
+            pltpu.VMEM((rank, LANES), jnp.float32),
             pltpu.SemaphoreType.DMA((slots,)),
             pltpu.SemaphoreType.DMA((2,)),
         ],

time: 53.5 us -> 52.2 us (0.976)
  Pallas kernels: 24.8 us -> 23.4 us
    pallas_call x1, Pallas kernels: 22.9 us -> 21.5 us  [stream(): pl.pallas_call(stream_kernel, out_shape=(pltpu.VMEM((rolls, span, LANES),...]
where the time goes in v3:
time: 52.2 us; the launch traced here: 52 us
  Pallas kernels  23.4 us (45%)
  waiting for transfers between devices  14.1 us (27%)
  starting transfers between devices  13.7 us (26%)
  between operations  0.71 us (1%)
    pallas_call x1, Pallas kernels, stream(): pl.pallas_call(stream_kernel, out_shape=(pltpu.VMEM((rolls, span, LANES),...  21.5 us
    ppermute x10, waiting for transfers between devices, swap(): lax.ppermute(value, axes, [(source, source ^ distance) for source in rang...  14.1 us
    ppermute x10, starting transfers between devices, swap(): lax.ppermute(value, axes, [(source, source ^ distance) for source in rang...  13.7 us
    pallas_call x1, Pallas kernels, update(): pl.pallas_call(functools.partial(update_kernel, scale), out_shape=(jax.Sh...  1.3 us
  transfers between devices with their start and end apart: 10, of which 10 were waited for; matrix products, arithmetic and copies ran while one was open for 0% of the time, Pallas kernels for 0%

profile of v3, /device:TPU:0, one launch (start us, length us, event | category | flops | bytes accessed | tf_op | source)
XLA Modules:
  0.0 52.0 jit_solution(12510152902909512371)
XLA Ops:
  0.6 0.0 copy-start
  0.6 21.5 %stream.1 = (f32[32,512,128]{2,1,0:T(8,128)S(1)}, f32[32,128]{1,0:T(8,128)S(1)}) custom-call(bf16[32,2048,512]{2,1,0:T(8,128)(2,1)} %density.1, bf16[32,2048]{1,0:T(8,128)(2,1)} %mach_hbm.1, bf16[32,512]{1,0:T(8,128)(2,1)} %cross_hbm.1), custom_call_target="tpu_custom_call" | custom-call | flops 2147483648 | bytes 67108864 | tf_op jit(solution)/shard_map/stream/pallas_call | solution.py:156
  22.2 4.0 %collective-permute-start.2 = (f32[32,128]{1,0:T(8,128)S(1)}, f32[32,128]{1,0:T(8,128)S(1)}, u32[]{:S(2)}, u32[]{:S(2)}) collective-permute-start(f32[32,128]{1,0:T(8,128)S(1)} %get-tuple-element.8), channel_id=1, source_target_pairs={{0,5},{1,4},{2,7},{3,6},{4,1},{5,0},{6,3},{7,2},{8,13},{9,12},{10,... | collective-permute-start | bytes 49160 | tf_op jit(solution)/shard_map/ppermute | solution.py:255
  26.2 0.5 collective-permute-start.1
  26.6 0.2 collective-permute-start
  26.8 1.1 %collective-permute-done.2 = f32[32,128]{1,0:T(8,128)S(1)} collective-permute-done((f32[32,128]{1,0:T(8,128)S(1)}, f32[32,128]{1,0:T(8,128)S(1)}, u32[]{:S(2)}, u32[]{:S(2)}) %collective-permute-start.2) | collective-permute-done | bytes 16416 | tf_op jit(solution)/shard_map/ppermute | solution.py:255
  27.9 2.0 %collective-permute-done.1 = f32[32,128]{1,0:T(8,128)S(1)} collective-permute-done((f32[32,128]{1,0:T(8,128)S(1)}, f32[32,128]{1,0:T(8,128)S(1)}, u32[]{:S(2)}, u32[]{:S(2)}) %collective-permute-start.1) | collective-permute-done | bytes 16416 | tf_op jit(solution)/shard_map/ppermute | solution.py:255
  29.9 0.5 collective-permute-done
  30.4 2.6 %collective-permute-start.3 = (f32[32,128]{1,0:T(8,128)S(1)}, f32[32,128]{1,0:T(8,128)S(1)}, u32[]{:S(2)}, u32[]{:S(2)}) collective-permute-start(f32[32,128]{1,0:T(8,128)S(1)} %add_add_fusion.1), channel_id=1, source_target_pairs={{0,2},{1,3},{2,0},{3,1},{4,6},{5,7},{6,4},{7,5},{8,10},{9,11},{10,... | collective-permute-start | bytes 49160 | tf_op jit(solution)/shard_map/ppermute | solution.py:255
  33.1 2.0 %collective-permute-done.3 = f32[32,128]{1,0:T(8,128)S(1)} collective-permute-done((f32[32,128]{1,0:T(8,128)S(1)}, f32[32,128]{1,0:T(8,128)S(1)}, u32[]{:S(2)}, u32[]{:S(2)}) %collective-permute-start.3) | collective-permute-done | bytes 16416 | tf_op jit(solution)/shard_map/ppermute | solution.py:255
  35.1 1.3 %update.1 = (f32[32,32]{1,0:T(8,128)}, f32[4,16,512]{2,1,0:T(8,128)S(1)}, f32[4,16,512]{2,1,0:T(8,128)S(1)}) custom-call(f32[32,512,128]{2,1,0:T(8,128)S(1)} %get-tuple-element.7.partial, f32[32,128]{1,0:T(8,128)S(1)} %select_add_fusion.payload, f32[32,32]{1,0:T(8,128)S(1)} %copy-done), custom_call_target="tpu_custom_call" | custom-call | flops 8388608 | tf_op jit(solution)/shard_map/update/pallas_call | solution.py:233
  36.4 0.1 collective-permute-start.4
  36.5 1.3 %collective-permute-done.4 = f32[4,16,512]{2,1,0:T(8,128)S(1)} collective-permute-done((f32[4,16,512]{2,1,0:T(8,128)S(1)}, f32[4,16,512]{2,1,0:T(8,128)S(1)}, u32[]{:S(2)}, u32[]{:S(2)}) %collective-permute-start.4) | collective-permute-done | bytes 131104 | tf_op jit(solution)/shard_map/ppermute | solution.py:255
  37.9 1.6 %collective-permute-start.6 = (f32[2,16,512]{2,1,0:T(8,128)S(1)}, f32[2,16,512]{2,1,0:T(8,128)S(1)}, u32[]{:S(2)}, u32[]{:S(2)}) collective-permute-start(f32[2,16,512]{2,1,0:T(8,128)S(1)} %get-tuple-element.12), channel_id=1, source_target_pairs={{0,16},{8,24},{16,0},{24,8},{1,17},{9,25},{17,1},{25,9},{2,18},{10... | collective-permute-start | bytes 196616 | tf_op jit(solution)/shard_map/ppermute | solution.py:255
  39.4 1.5 %collective-permute-start.7 = (f32[2,16,512]{2,1,0:T(8,128)S(1)}, f32[2,16,512]{2,1,0:T(8,128)S(1)}, u32[]{:S(2)}, u32[]{:S(2)}) collective-permute-start(f32[2,16,512]{2,1,0:T(8,128)S(1)} %get-tuple-element.13), channel_id=1, source_target_pairs={{0,17},{1,16},{2,19},{3,18},{8,25},{9,24},{10,27},{11,26},{16,1},{... | collective-permute-start | bytes 196616 | tf_op jit(solution)/shard_map/ppermute | solution.py:255
  41.0 0.5 collective-permute-start.5
  41.4 0.8 %collective-permute-done.6 = f32[2,16,512]{2,1,0:T(8,128)S(1)} collective-permute-done((f32[2,16,512]{2,1,0:T(8,128)S(1)}, f32[2,16,512]{2,1,0:T(8,128)S(1)}, u32[]{:S(2)}, u32[]{:S(2)}) %collective-permute-start.6) | collective-permute-done | bytes 65568 | tf_op jit(solution)/shard_map/ppermute | solution.py:255
  42.2 2.9 %collective-permute-done.7 = f32[2,16,512]{2,1,0:T(8,128)S(1)} collective-permute-done((f32[2,16,512]{2,1,0:T(8,128)S(1)}, f32[2,16,512]{2,1,0:T(8,128)S(1)}, u32[]{:S(2)}, u32[]{:S(2)}) %collective-permute-start.7) | collective-permute-done | bytes 65568 | tf_op jit(solution)/shard_map/ppermute | solution.py:255
  45.1 0.1 collective-permute-done.5
  45.3 2.7 %collective-permute-start.8 = (f32[16,512]{1,0:T(8,128)S(1)}, f32[16,512]{1,0:T(8,128)S(1)}, u32[]{:S(2)}, u32[]{:S(2)}) collective-permute-start(f32[16,512]{1,0:T(8,128)S(1)} %slice_bitcast_fusion), channel_id=1, source_target_pairs={{0,2},{1,3},{2,0},{3,1},{4,6},{5,7},{6,4},{7,5},{8,10},{9,11},{10,... | collective-permute-start | bytes 98312 | tf_op jit(solution)/shard_map/ppermute | solution.py:255
  48.0 2.2 %collective-permute-done.8 = f32[16,512]{1,0:T(8,128)S(1)} collective-permute-done((f32[16,512]{1,0:T(8,128)S(1)}, f32[16,512]{1,0:T(8,128)S(1)}, u32[]{:S(2)}, u32[]{:S(2)}) %collective-permute-start.8) | collective-permute-done | bytes 32800 | tf_op jit(solution)/shard_map/ppermute | solution.py:255
  50.2 0.0 collective-permute-start.9
  50.2 1.2 %collective-permute-done.9.other = f32[16,512]{1,0:T(8,128)S(1)} collective-permute-done((f32[16,512]{1,0:T(8,128)S(1)}, f32[16,512]{1,0:T(8,128)S(1)}, u32[]{:S(2)}, u32[]{:S(2)}) %collective-permute-start.9) | collective-permute-done | bytes 32800 | tf_op jit(solution)/shard_map/ppermute | solution.py:255
  51.4 0.6 %join.1 = f32[32,512]{1,0:T(8,128)} custom-call(f32[16,512]{1,0:T(8,128)S(1)} %fusion.own, f32[16,512]{1,0:T(8,128)S(1)} %collective-permute-done.9.other), custom_call_target="tpu_custom_call" | custom-call | tf_op jit(solution)/shard_map/join/pallas_call | solution.py:312
  (11 shorter events, 0.1 us)
Async XLA Ops:
  0.6 34.5 %copy-start = (f32[32,32]{1,0:T(8,128)S(1)}, f32[32,32]{1,0:T(8,128)}, u32[]{:S(2)}) copy-start(f32[32,32]{1,0:T(8,128)} %start.1) | copy-start | bytes 12292
  22.2 5.8 %collective-permute-start.2 = (f32[32,128]{1,0:T(8,128)S(1)}, f32[32,128]{1,0:T(8,128)S(1)}, u32[]{:S(2)}, u32[]{:S(2)}) collective-permute-start(f32[32,128]{1,0:T(8,128)S(1)} %get-tuple-element.8), channel_id=1, source_target_pairs={{0,5},{1,4},{2,7},{3,6},{4,1},{5,0},{6,3},{7,2},{8,13},{9,12},{10,... | collective-permute-start | bytes 49160 | tf_op jit(solution)/shard_map/ppermute | solution.py:255
  26.2 3.7 %collective-permute-start.1 = (f32[32,128]{1,0:T(8,128)S(1)}, f32[32,128]{1,0:T(8,128)S(1)}, u32[]{:S(2)}, u32[]{:S(2)}) collective-permute-start(f32[32,128]{1,0:T(8,128)S(1)} %get-tuple-element.8), channel_id=1, source_target_pairs={{0,1},{1,0},{2,3},{3,2},{4,5},{5,4},{6,7},{7,6},{8,9},{9,8},{10,11... | collective-permute-start | bytes 49160 | tf_op jit(solution)/shard_map/ppermute | solution.py:255
  26.6 3.7 %collective-permute-start = (f32[32,128]{1,0:T(8,128)S(1)}, f32[32,128]{1,0:T(8,128)S(1)}, u32[]{:S(2)}, u32[]{:S(2)}) collective-permute-start(f32[32,128]{1,0:T(8,128)S(1)} %get-tuple-element.8), channel_id=1, source_target_pairs={{0,4},{1,5},{2,6},{3,7},{4,0},{5,1},{6,2},{7,3},{8,12},{9,13},{10,... | collective-permute-start | bytes 49160 | tf_op jit(solution)/shard_map/ppermute | solution.py:255
  30.4 4.7 %collective-permute-start.3 = (f32[32,128]{1,0:T(8,128)S(1)}, f32[32,128]{1,0:T(8,128)S(1)}, u32[]{:S(2)}, u32[]{:S(2)}) collective-permute-start(f32[32,128]{1,0:T(8,128)S(1)} %add_add_fusion.1), channel_id=1, source_target_pairs={{0,2},{1,3},{2,0},{3,1},{4,6},{5,7},{6,4},{7,5},{8,10},{9,11},{10,... | collective-permute-start | bytes 49160 | tf_op jit(solution)/shard_map/ppermute | solution.py:255
  36.4 1.4 %collective-permute-start.4 = (f32[4,16,512]{2,1,0:T(8,128)S(1)}, f32[4,16,512]{2,1,0:T(8,128)S(1)}, u32[]{:S(2)}, u32[]{:S(2)}) collective-permute-start(f32[4,16,512]{2,1,0:T(8,128)S(1)} %get-tuple-element.11), channel_id=1, source_target_pairs={{0,8},{8,0},{16,24},{24,16},{1,9},{9,1},{17,25},{25,17},{2,10},{10... | collective-permute-start | bytes 393224 | tf_op jit(solution)/shard_map/ppermute | solution.py:255
  37.9 4.3 %collective-permute-start.6 = (f32[2,16,512]{2,1,0:T(8,128)S(1)}, f32[2,16,512]{2,1,0:T(8,128)S(1)}, u32[]{:S(2)}, u32[]{:S(2)}) collective-permute-start(f32[2,16,512]{2,1,0:T(8,128)S(1)} %get-tuple-element.12), channel_id=1, source_target_pairs={{0,16},{8,24},{16,0},{24,8},{1,17},{9,25},{17,1},{25,9},{2,18},{10... | collective-permute-start | bytes 196616 | tf_op jit(solution)/shard_map/ppermute | solution.py:255
  39.4 5.7 %collective-permute-start.7 = (f32[2,16,512]{2,1,0:T(8,128)S(1)}, f32[2,16,512]{2,1,0:T(8,128)S(1)}, u32[]{:S(2)}, u32[]{:S(2)}) collective-permute-start(f32[2,16,512]{2,1,0:T(8,128)S(1)} %get-tuple-element.13), channel_id=1, source_target_pairs={{0,17},{1,16},{2,19},{3,18},{8,25},{9,24},{10,27},{11,26},{16,1},{... | collective-permute-start | bytes 196616 | tf_op jit(solution)/shard_map/ppermute | solution.py:255
  41.0 4.3 %collective-permute-start.5 = (f32[2,16,512]{2,1,0:T(8,128)S(1)}, f32[2,16,512]{2,1,0:T(8,128)S(1)}, u32[]{:S(2)}, u32[]{:S(2)}) collective-permute-start(f32[2,16,512]{2,1,0:T(8,128)S(1)} %get-tuple-element.13), channel_id=1, source_target_pairs={{0,1},{1,0},{2,3},{3,2},{4,5},{5,4},{6,7},{7,6},{8,9},{9,8},{10,11... | collective-permute-start | bytes 196616 | tf_op jit(solution)/shard_map/ppermute | solution.py:255
  45.3 4.9 %collective-permute-start.8 = (f32[16,512]{1,0:T(8,128)S(1)}, f32[16,512]{1,0:T(8,128)S(1)}, u32[]{:S(2)}, u32[]{:S(2)}) collective-permute-start(f32[16,512]{1,0:T(8,128)S(1)} %slice_bitcast_fusion), channel_id=1, source_target_pairs={{0,2},{1,3},{2,0},{3,1},{4,6},{5,7},{6,4},{7,5},{8,10},{9,11},{10,... | collective-permute-start | bytes 98312 | tf_op jit(solution)/shard_map/ppermute | solution.py:255
  50.2 1.2 %collective-permute-start.9 = (f32[16,512]{1,0:T(8,128)S(1)}, f32[16,512]{1,0:T(8,128)S(1)}, u32[]{:S(2)}, u32[]{:S(2)}) collective-permute-start(f32[16,512]{1,0:T(8,128)S(1)} %fusion.own), channel_id=1, source_target_pairs={{0,8},{8,0},{16,24},{24,16},{1,9},{9,1},{17,25},{25,17},{2,10},{10... | collective-permute-start | bytes 98312 | tf_op jit(solution)/shard_map/ppermute | solution.py:255

commit v4 on v3

--- a/solution.py
+++ b/solution.py
@@ -182,7 +182,7 @@
     )(density, in_hbm(mach), in_hbm(cross))
 
 
-def update_kernel(scale, partial, payload, start, roll_out, keep, send, total, blocks, roll_rows, sem):
+def update_kernel(scale, partial, payload, start, roll_out, keep, send, total, blocks, roll_rows, share_wide):
     rolls, span, lanes = partial.shape
     rank = start.shape[0]
     groups = lanes // rank
@@ -194,19 +194,21 @@
     diag = jnp.sum(jnp.where(row_id == lane_id, gram, 0.0), axis=1, keepdims=True)
     share = gram / diag
     rows = start[...]
-    gap = flipped[0:rank] / diag
+    upper = jnp.where(lane_id > row_id, share, 0.0)
+    scaled = flipped[0:rank] / diag
     for r in range(rank):
-        gap = gap - share[:, r : r + 1] * rows[r : r + 1, :]
+        share_wide[r] = jnp.broadcast_to(share[:, r : r + 1], (rank, rolls))
+    old = jnp.dot(upper, rows, precision=lax.Precision.HIGHEST, preferred_element_type=jnp.float32)
+    roll_rows[...] = scaled - old
+    gap = [roll_rows[r : r + 1, :] for r in range(rank)]
     done = []
     for r in range(rank):
-        current = rows[r : r + 1, :]
-        updated = jnp.maximum(current + gap[r : r + 1, :], 0.0)
-        gap = gap - share[:, r : r + 1] * (updated - current)
+        updated = jnp.maximum(gap[r], 0.0)
+        for later in range(r + 1, rank):
+            gap[later] = gap[later] - share_wide[r, later : later + 1, :] * updated
         done.append(updated)
     factor = jnp.concatenate(done, axis=0)
-    roll_rows[...] = factor
-    store = pltpu.make_async_copy(roll_rows, roll_out, sem)
-    store.start()
+    roll_out[...] = factor
     factor_lanes = jnp.concatenate([factor * scale] * groups, axis=0).T
 
     chunk = min(span, 64)
@@ -221,8 +223,6 @@
     for slot, distance in enumerate((0, 2, 1, 3)):
         keep[slot] = blocks[cross_at ^ distance, core]
         send[slot] = blocks[cross_at ^ distance, 1 - core]
-    store.wait()
-
 
 def update(scale, partial, payload, start):
     rolls, span, lanes = partial.shape
@@ -232,14 +232,14 @@
     part = pltpu.VMEM((groups, rank // 2, span), jnp.float32)
     return pl.pallas_call(
         functools.partial(update_kernel, scale),
-        out_shape=(jax.ShapeDtypeStruct((rank, rolls), jnp.float32), part, part),
+        out_shape=(pltpu.VMEM((rank, rolls), jnp.float32), part, part),
         in_specs=[vmem, vmem, vmem],
-        out_specs=(pl.BlockSpec(memory_space=pl.ANY), vmem, vmem),
+        out_specs=(vmem, vmem, vmem),
         scratch_shapes=[
             pltpu.VMEM((span, lanes), jnp.float32),
             pltpu.VMEM((groups, 2, rank // 2, span), jnp.float32),
             pltpu.VMEM((rank, rolls), jnp.float32),
-            pltpu.SemaphoreType.DMA,
+            pltpu.VMEM((rank, rank, rolls), jnp.float32),
         ],
         compiler_params=pltpu.CompilerParams(vmem_limit_bytes=40 * MIB),
         cost_estimate=pl.CostEstimate(flops=4 * rolls * span * lanes, bytes_accessed=0, transcendentals=0),
@@ -293,31 +293,38 @@
     by_both = swap(his, ("roll", "cross"), 2 * cross_size + 1)
     value = mine + (by_cross + (by_roll + by_both))
     value = value[0] + swap(value[1], "cross", 2)
-    return join(value, swap(value, "roll", 1))
-
-
-def join_kernel(own, other, out, sem):
+    return value, swap(value, "roll", 1)
+
+
+def join_kernel(own, other, factor, factor_out, out, sem):
     core = lax.rem(lax.axis_index("roll"), 2)
     half = own.shape[0]
-    first = pltpu.make_async_copy(own, out.at[pl.ds(pl.multiple_of(core * half, half), half)], sem.at[0])
-    second = pltpu.make_async_copy(other, out.at[pl.ds(pl.multiple_of((1 - core) * half, half), half)], sem.at[1])
-    first.start()
-    second.start()
-    first.wait()
-    second.wait()
-
-
-def join(own, other):
+    stores = (
+        pltpu.make_async_copy(own, out.at[pl.ds(pl.multiple_of(core * half, half), half)], sem.at[0]),
+        pltpu.make_async_copy(other, out.at[pl.ds(pl.multiple_of((1 - core) * half, half), half)], sem.at[1]),
+        pltpu.make_async_copy(factor, factor_out, sem.at[2]),
+    )
+    for store in stores:
+        store.start()
+    for store in stores:
+        store.wait()
+
+
+def join(own, other, factor):
     vmem = pl.BlockSpec(memory_space=pltpu.VMEM)
+    anywhere = pl.BlockSpec(memory_space=pl.ANY)
     return pl.pallas_call(
         join_kernel,
-        out_shape=jax.ShapeDtypeStruct((2 * own.shape[0], own.shape[1]), own.dtype),
-        in_specs=[vmem, vmem],
-        out_specs=pl.BlockSpec(memory_space=pl.ANY),
-        scratch_shapes=[pltpu.SemaphoreType.DMA((2,))],
+        out_shape=(
+            jax.ShapeDtypeStruct(factor.shape, factor.dtype),
+            jax.ShapeDtypeStruct((2 * own.shape[0], own.shape[1]), own.dtype),
+        ),
+        in_specs=[vmem, vmem, vmem],
+        out_specs=(anywhere, anywhere),
+        scratch_shapes=[pltpu.SemaphoreType.DMA((3,))],
         compiler_params=pltpu.CompilerParams(vmem_limit_bytes=8 * MIB),
         name="join",
-    )(own, other)
+    )(own, other, factor)
 
 
 def local(density, roll_start, mach_factor, cross_factor):
@@ -329,7 +336,8 @@
     partial_value, payload = stream(density, mach_factor, cross_factor)
     payload = reduce_payload(payload, rank)
     roll_factor, keep, send = update(scale, partial_value, payload, roll_start)
-    return (roll_factor, reduce_blocks(keep, send))
+    own, other = reduce_blocks(keep, send)
+    return join(own, other, roll_factor)
 
 
 def solution(mesh):

time: 52.2 us -> 52.1 us (level)
  no operation moved by 1% of the time
where the time goes in v4:
time: 52.1 us; the launch traced here: 51.9 us
  Pallas kernels  23.3 us (45%)
  waiting for transfers between devices  14.1 us (27%)
  starting transfers between devices  13.7 us (26%)
  between operations  0.7 us (1%)
    pallas_call x1, Pallas kernels, stream(): pl.pallas_call(stream_kernel, out_shape=(pltpu.VMEM((rolls, span, LANES),...  21.5 us
    ppermute x10, waiting for transfers between devices, swap(): lax.ppermute(value, axes, [(source, source ^ distance) for source in rang...  14.1 us
    ppermute x10, starting transfers between devices, swap(): lax.ppermute(value, axes, [(source, source ^ distance) for source in rang...  13.7 us
    pallas_call x1, Pallas kernels, update(): pl.pallas_call(functools.partial(update_kernel, scale), out_shape=(pltpu....  1.19 us
  transfers between devices with their start and end apart: 10, of which 10 were waited for; matrix products, arithmetic and copies ran while one was open for 0% of the time, Pallas kernels for 0%

profile of v4, /device:TPU:0, one launch (start us, length us, event | category | flops | bytes accessed | tf_op | source)
XLA Modules:
  0.0 51.9 jit_solution(10255035240842023936)
XLA Ops:
  0.6 0.0 copy-start
  0.6 21.5 %stream.1 = (f32[32,512,128]{2,1,0:T(8,128)S(1)}, f32[32,128]{1,0:T(8,128)S(1)}) custom-call(bf16[32,2048,512]{2,1,0:T(8,128)(2,1)} %density.1, bf16[32,2048]{1,0:T(8,128)(2,1)} %mach_hbm.1, bf16[32,512]{1,0:T(8,128)(2,1)} %cross_hbm.1), custom_call_target="tpu_custom_call" | custom-call | flops 2147483648 | bytes 67108864 | tf_op jit(solution)/shard_map/stream/pallas_call | solution.py:156
  22.2 4.0 %collective-permute-start.2 = (f32[32,128]{1,0:T(8,128)S(1)}, f32[32,128]{1,0:T(8,128)S(1)}, u32[]{:S(2)}, u32[]{:S(2)}) collective-permute-start(f32[32,128]{1,0:T(8,128)S(1)} %get-tuple-element.8), channel_id=1, source_target_pairs={{0,5},{1,4},{2,7},{3,6},{4,1},{5,0},{6,3},{7,2},{8,13},{9,12},{10,... | collective-permute-start | bytes 49160 | tf_op jit(solution)/shard_map/ppermute | solution.py:255
  26.2 0.5 collective-permute-start.1
  26.6 0.2 collective-permute-start
  26.8 1.1 %collective-permute-done.2 = f32[32,128]{1,0:T(8,128)S(1)} collective-permute-done((f32[32,128]{1,0:T(8,128)S(1)}, f32[32,128]{1,0:T(8,128)S(1)}, u32[]{:S(2)}, u32[]{:S(2)}) %collective-permute-start.2) | collective-permute-done | bytes 16416 | tf_op jit(solution)/shard_map/ppermute | solution.py:255
  27.9 2.0 %collective-permute-done.1 = f32[32,128]{1,0:T(8,128)S(1)} collective-permute-done((f32[32,128]{1,0:T(8,128)S(1)}, f32[32,128]{1,0:T(8,128)S(1)}, u32[]{:S(2)}, u32[]{:S(2)}) %collective-permute-start.1) | collective-permute-done | bytes 16416 | tf_op jit(solution)/shard_map/ppermute | solution.py:255
  29.9 0.5 collective-permute-done
  30.4 2.6 %collective-permute-start.3 = (f32[32,128]{1,0:T(8,128)S(1)}, f32[32,128]{1,0:T(8,128)S(1)}, u32[]{:S(2)}, u32[]{:S(2)}) collective-permute-start(f32[32,128]{1,0:T(8,128)S(1)} %add_add_fusion.1), channel_id=1, source_target_pairs={{0,2},{1,3},{2,0},{3,1},{4,6},{5,7},{6,4},{7,5},{8,10},{9,11},{10,... | collective-permute-start | bytes 49160 | tf_op jit(solution)/shard_map/ppermute | solution.py:255
  33.1 2.0 %collective-permute-done.3 = f32[32,128]{1,0:T(8,128)S(1)} collective-permute-done((f32[32,128]{1,0:T(8,128)S(1)}, f32[32,128]{1,0:T(8,128)S(1)}, u32[]{:S(2)}, u32[]{:S(2)}) %collective-permute-start.3) | collective-permute-done | bytes 16416 | tf_op jit(solution)/shard_map/ppermute | solution.py:255
  35.1 1.2 %update.1 = (f32[32,32]{1,0:T(8,128)S(1)}, f32[4,16,512]{2,1,0:T(8,128)S(1)}, f32[4,16,512]{2,1,0:T(8,128)S(1)}) custom-call(f32[32,512,128]{2,1,0:T(8,128)S(1)} %get-tuple-element.7.partial, f32[32,128]{1,0:T(8,128)S(1)} %select_add_fusion.payload, f32[32,32]{1,0:T(8,128)S(1)} %copy-done), custom_call_target="tpu_custom_call" | custom-call | flops 8388608 | tf_op jit(solution)/shard_map/update/pallas_call | solution.py:233
  36.3 0.1 collective-permute-start.4
  36.4 1.3 %collective-permute-done.4 = f32[4,16,512]{2,1,0:T(8,128)S(1)} collective-permute-done((f32[4,16,512]{2,1,0:T(8,128)S(1)}, f32[4,16,512]{2,1,0:T(8,128)S(1)}, u32[]{:S(2)}, u32[]{:S(2)}) %collective-permute-start.4) | collective-permute-done | bytes 131104 | tf_op jit(solution)/shard_map/ppermute | solution.py:255
  37.8 1.6 %collective-permute-start.6 = (f32[2,16,512]{2,1,0:T(8,128)S(1)}, f32[2,16,512]{2,1,0:T(8,128)S(1)}, u32[]{:S(2)}, u32[]{:S(2)}) collective-permute-start(f32[2,16,512]{2,1,0:T(8,128)S(1)} %get-tuple-element.12), channel_id=1, source_target_pairs={{0,16},{8,24},{16,0},{24,8},{1,17},{9,25},{17,1},{25,9},{2,18},{10... | collective-permute-start | bytes 196616 | tf_op jit(solution)/shard_map/ppermute | solution.py:255
  39.3 1.5 %collective-permute-start.7 = (f32[2,16,512]{2,1,0:T(8,128)S(1)}, f32[2,16,512]{2,1,0:T(8,128)S(1)}, u32[]{:S(2)}, u32[]{:S(2)}) collective-permute-start(f32[2,16,512]{2,1,0:T(8,128)S(1)} %get-tuple-element.13), channel_id=1, source_target_pairs={{0,17},{1,16},{2,19},{3,18},{8,25},{9,24},{10,27},{11,26},{16,1},{... | collective-permute-start | bytes 196616 | tf_op jit(solution)/shard_map/ppermute | solution.py:255
  40.9 0.5 collective-permute-start.5
  41.3 0.8 %collective-permute-done.6 = f32[2,16,512]{2,1,0:T(8,128)S(1)} collective-permute-done((f32[2,16,512]{2,1,0:T(8,128)S(1)}, f32[2,16,512]{2,1,0:T(8,128)S(1)}, u32[]{:S(2)}, u32[]{:S(2)}) %collective-permute-start.6) | collective-permute-done | bytes 65568 | tf_op jit(solution)/shard_map/ppermute | solution.py:255
  42.1 2.9 %collective-permute-done.7 = f32[2,16,512]{2,1,0:T(8,128)S(1)} collective-permute-done((f32[2,16,512]{2,1,0:T(8,128)S(1)}, f32[2,16,512]{2,1,0:T(8,128)S(1)}, u32[]{:S(2)}, u32[]{:S(2)}) %collective-permute-start.7) | collective-permute-done | bytes 65568 | tf_op jit(solution)/shard_map/ppermute | solution.py:255
  45.0 0.1 collective-permute-done.5
  45.2 2.7 %collective-permute-start.8 = (f32[16,512]{1,0:T(8,128)S(1)}, f32[16,512]{1,0:T(8,128)S(1)}, u32[]{:S(2)}, u32[]{:S(2)}) collective-permute-start(f32[16,512]{1,0:T(8,128)S(1)} %slice_bitcast_fusion), channel_id=1, source_target_pairs={{0,2},{1,3},{2,0},{3,1},{4,6},{5,7},{6,4},{7,5},{8,10},{9,11},{10,... | collective-permute-start | bytes 98312 | tf_op jit(solution)/shard_map/ppermute | solution.py:255
  47.9 2.2 %collective-permute-done.8 = f32[16,512]{1,0:T(8,128)S(1)} collective-permute-done((f32[16,512]{1,0:T(8,128)S(1)}, f32[16,512]{1,0:T(8,128)S(1)}, u32[]{:S(2)}, u32[]{:S(2)}) %collective-permute-start.8) | collective-permute-done | bytes 32800 | tf_op jit(solution)/shard_map/ppermute | solution.py:255
  50.0 0.0 collective-permute-start.9
  50.1 1.2 %collective-permute-done.9.other = f32[16,512]{1,0:T(8,128)S(1)} collective-permute-done((f32[16,512]{1,0:T(8,128)S(1)}, f32[16,512]{1,0:T(8,128)S(1)}, u32[]{:S(2)}, u32[]{:S(2)}) %collective-permute-start.9) | collective-permute-done | bytes 32800 | tf_op jit(solution)/shard_map/ppermute | solution.py:255
  51.3 0.7 %join.1 = (f32[32,32]{1,0:T(8,128)}, f32[32,512]{1,0:T(8,128)}) custom-call(f32[16,512]{1,0:T(8,128)S(1)} %fusion.own, f32[16,512]{1,0:T(8,128)S(1)} %collective-permute-done.9.other, f32[32,32]{1,0:T(8,128)S(1)} %get-tuple-element.11.factor), custom_call_target="tpu_custom_call" | custom-call | tf_op jit(solution)/shard_map/join/pallas_call | solution.py:316
  (11 shorter events, 0.1 us)
Async XLA Ops:
  0.6 34.5 %copy-start = (f32[32,32]{1,0:T(8,128)S(1)}, f32[32,32]{1,0:T(8,128)}, u32[]{:S(2)}) copy-start(f32[32,32]{1,0:T(8,128)} %start.1) | copy-start | bytes 12292
  22.2 5.8 %collective-permute-start.2 = (f32[32,128]{1,0:T(8,128)S(1)}, f32[32,128]{1,0:T(8,128)S(1)}, u32[]{:S(2)}, u32[]{:S(2)}) collective-permute-start(f32[32,128]{1,0:T(8,128)S(1)} %get-tuple-element.8), channel_id=1, source_target_pairs={{0,5},{1,4},{2,7},{3,6},{4,1},{5,0},{6,3},{7,2},{8,13},{9,12},{10,... | collective-permute-start | bytes 49160 | tf_op jit(solution)/shard_map/ppermute | solution.py:255
  26.2 3.7 %collective-permute-start.1 = (f32[32,128]{1,0:T(8,128)S(1)}, f32[32,128]{1,0:T(8,128)S(1)}, u32[]{:S(2)}, u32[]{:S(2)}) collective-permute-start(f32[32,128]{1,0:T(8,128)S(1)} %get-tuple-element.8), channel_id=1, source_target_pairs={{0,1},{1,0},{2,3},{3,2},{4,5},{5,4},{6,7},{7,6},{8,9},{9,8},{10,11... | collective-permute-start | bytes 49160 | tf_op jit(solution)/shard_map/ppermute | solution.py:255
  26.6 3.7 %collective-permute-start = (f32[32,128]{1,0:T(8,128)S(1)}, f32[32,128]{1,0:T(8,128)S(1)}, u32[]{:S(2)}, u32[]{:S(2)}) collective-permute-start(f32[32,128]{1,0:T(8,128)S(1)} %get-tuple-element.8), channel_id=1, source_target_pairs={{0,4},{1,5},{2,6},{3,7},{4,0},{5,1},{6,2},{7,3},{8,12},{9,13},{10,... | collective-permute-start | bytes 49160 | tf_op jit(solution)/shard_map/ppermute | solution.py:255
  30.4 4.7 %collective-permute-start.3 = (f32[32,128]{1,0:T(8,128)S(1)}, f32[32,128]{1,0:T(8,128)S(1)}, u32[]{:S(2)}, u32[]{:S(2)}) collective-permute-start(f32[32,128]{1,0:T(8,128)S(1)} %add_add_fusion.1), channel_id=1, source_target_pairs={{0,2},{1,3},{2,0},{3,1},{4,6},{5,7},{6,4},{7,5},{8,10},{9,11},{10,... | collective-permute-start | bytes 49160 | tf_op jit(solution)/shard_map/ppermute | solution.py:255
  36.3 1.4 %collective-permute-start.4 = (f32[4,16,512]{2,1,0:T(8,128)S(1)}, f32[4,16,512]{2,1,0:T(8,128)S(1)}, u32[]{:S(2)}, u32[]{:S(2)}) collective-permute-start(f32[4,16,512]{2,1,0:T(8,128)S(1)} %get-tuple-element.10), channel_id=1, source_target_pairs={{0,8},{8,0},{16,24},{24,16},{1,9},{9,1},{17,25},{25,17},{2,10},{10... | collective-permute-start | bytes 393224 | tf_op jit(solution)/shard_map/ppermute | solution.py:255
  37.8 4.3 %collective-permute-start.6 = (f32[2,16,512]{2,1,0:T(8,128)S(1)}, f32[2,16,512]{2,1,0:T(8,128)S(1)}, u32[]{:S(2)}, u32[]{:S(2)}) collective-permute-start(f32[2,16,512]{2,1,0:T(8,128)S(1)} %get-tuple-element.12), channel_id=1, source_target_pairs={{0,16},{8,24},{16,0},{24,8},{1,17},{9,25},{17,1},{25,9},{2,18},{10... | collective-permute-start | bytes 196616 | tf_op jit(solution)/shard_map/ppermute | solution.py:255
  39.3 5.7 %collective-permute-start.7 = (f32[2,16,512]{2,1,0:T(8,128)S(1)}, f32[2,16,512]{2,1,0:T(8,128)S(1)}, u32[]{:S(2)}, u32[]{:S(2)}) collective-permute-start(f32[2,16,512]{2,1,0:T(8,128)S(1)} %get-tuple-element.13), channel_id=1, source_target_pairs={{0,17},{1,16},{2,19},{3,18},{8,25},{9,24},{10,27},{11,26},{16,1},{... | collective-permute-start | bytes 196616 | tf_op jit(solution)/shard_map/ppermute | solution.py:255
  40.9 4.3 %collective-permute-start.5 = (f32[2,16,512]{2,1,0:T(8,128)S(1)}, f32[2,16,512]{2,1,0:T(8,128)S(1)}, u32[]{:S(2)}, u32[]{:S(2)}) collective-permute-start(f32[2,16,512]{2,1,0:T(8,128)S(1)} %get-tuple-element.13), channel_id=1, source_target_pairs={{0,1},{1,0},{2,3},{3,2},{4,5},{5,4},{6,7},{7,6},{8,9},{9,8},{10,11... | collective-permute-start | bytes 196616 | tf_op jit(solution)/shard_map/ppermute | solution.py:255
  45.2 4.9 %collective-permute-start.8 = (f32[16,512]{1,0:T(8,128)S(1)}, f32[16,512]{1,0:T(8,128)S(1)}, u32[]{:S(2)}, u32[]{:S(2)}) collective-permute-start(f32[16,512]{1,0:T(8,128)S(1)} %slice_bitcast_fusion), channel_id=1, source_target_pairs={{0,2},{1,3},{2,0},{3,1},{4,6},{5,7},{6,4},{7,5},{8,10},{9,11},{10,... | collective-permute-start | bytes 98312 | tf_op jit(solution)/shard_map/ppermute | solution.py:255
  50.0 1.2 %collective-permute-start.9 = (f32[16,512]{1,0:T(8,128)S(1)}, f32[16,512]{1,0:T(8,128)S(1)}, u32[]{:S(2)}, u32[]{:S(2)}) collective-permute-start(f32[16,512]{1,0:T(8,128)S(1)} %fusion.own), channel_id=1, source_target_pairs={{0,8},{8,0},{16,24},{24,16},{1,9},{9,1},{17,25},{25,17},{2,10},{10... | collective-permute-start | bytes 98312 | tf_op jit(solution)/shard_map/ppermute | solution.py:255

commit v5 on v4

--- a/solution.py
+++ b/solution.py
@@ -182,11 +182,32 @@
     )(density, in_hbm(mach), in_hbm(cross))
 
 
-def update_kernel(scale, partial, payload, start, roll_out, keep, send, total, blocks, roll_rows, share_wide):
+def half_term(partial, factor_lanes, half, out, total, blocks):
+    rolls, span, _ = partial.shape
+    groups, rank, bins = blocks.shape
+    chunk = min(bins, 64)
+    for first in range(0, bins, chunk):
+        rows = pl.ds(pl.multiple_of(half * bins + first, chunk), chunk)
+        value = partial[0, rows, :] * factor_lanes[0:1, :]
+        for roll in range(1, rolls):
+            value = value + partial[roll, rows, :] * factor_lanes[roll : roll + 1, :]
+        total[first : first + chunk, :] = value
+    blocks[...] = total[...].T.reshape(groups, rank, bins)
+    cross_at = lax.axis_index("cross")
+    for slot, distance in enumerate((0, 2, 1, 3)):
+        out[slot] = blocks[cross_at ^ distance]
+
+
+def this_core():
+    return lax.rem(lax.axis_index("roll"), 2)
+
+
+def update_kernel(
+    scale, partial, payload, start, roll_out, lanes_out, send, total, blocks, roll_rows, share_wide
+):
     rolls, span, lanes = partial.shape
     rank = start.shape[0]
     groups = lanes // rank
-    half = rank // 2
     flipped = payload[...].T
     gram = flipped[rank : 2 * rank] * flipped[2 * rank : 3 * rank]
     row_id = lax.broadcasted_iota(jnp.int32, (rank, rank), 0)
@@ -210,41 +231,53 @@
     factor = jnp.concatenate(done, axis=0)
     roll_out[...] = factor
     factor_lanes = jnp.concatenate([factor * scale] * groups, axis=0).T
-
-    chunk = min(span, 64)
-    for first in range(0, span, chunk):
-        value = partial[0, first : first + chunk, :] * factor_lanes[0:1, :]
-        for roll in range(1, rolls):
-            value = value + partial[roll, first : first + chunk, :] * factor_lanes[roll : roll + 1, :]
-        total[first : first + chunk, :] = value
-    blocks[...] = total[...].T.reshape(groups, 2, half, span)
-    core = lax.rem(lax.axis_index("roll"), 2)
-    cross_at = lax.axis_index("cross")
-    for slot, distance in enumerate((0, 2, 1, 3)):
-        keep[slot] = blocks[cross_at ^ distance, core]
-        send[slot] = blocks[cross_at ^ distance, 1 - core]
+    lanes_out[...] = factor_lanes
+    half_term(partial, factor_lanes, 1 - this_core(), send, total, blocks)
+
+
+def keep_kernel(partial, factor_lanes, keep, total, blocks):
+    half_term(partial, factor_lanes[...], this_core(), keep, total, blocks)
+
 
 def update(scale, partial, payload, start):
     rolls, span, lanes = partial.shape
     rank = start.shape[0]
-    groups = lanes // rank
     vmem = pl.BlockSpec(memory_space=pltpu.VMEM)
-    part = pltpu.VMEM((groups, rank // 2, span), jnp.float32)
-    return pl.pallas_call(
+    in_vmem = functools.partial(pltpu.with_memory_space_constraint, memory_space=pltpu.VMEM)
+    partial = in_vmem(partial)
+    part = pltpu.VMEM((lanes // rank, rank, span // 2), jnp.float32)
+    work = [
+        pltpu.VMEM((span // 2, lanes), jnp.float32),
+        pltpu.VMEM((lanes // rank, rank, span // 2), jnp.float32),
+    ]
+    cost = pl.CostEstimate(flops=rolls * span * lanes, bytes_accessed=0, transcendentals=0)
+    roll_factor, factor_lanes, send = pl.pallas_call(
         functools.partial(update_kernel, scale),
-        out_shape=(pltpu.VMEM((rank, rolls), jnp.float32), part, part),
+        out_shape=(
+            pltpu.VMEM((rank, rolls), jnp.float32),
+            pltpu.VMEM((rolls, lanes), jnp.float32),
+            part,
+        ),
         in_specs=[vmem, vmem, vmem],
         out_specs=(vmem, vmem, vmem),
-        scratch_shapes=[
-            pltpu.VMEM((span, lanes), jnp.float32),
-            pltpu.VMEM((groups, 2, rank // 2, span), jnp.float32),
-            pltpu.VMEM((rank, rolls), jnp.float32),
-            pltpu.VMEM((rank, rank, rolls), jnp.float32),
-        ],
+        scratch_shapes=work
+        + [pltpu.VMEM((rank, rolls), jnp.float32), pltpu.VMEM((rank, rank, rolls), jnp.float32)],
         compiler_params=pltpu.CompilerParams(vmem_limit_bytes=40 * MIB),
-        cost_estimate=pl.CostEstimate(flops=4 * rolls * span * lanes, bytes_accessed=0, transcendentals=0),
+        cost_estimate=cost,
         name="update",
-    )(pltpu.with_memory_space_constraint(partial, pltpu.VMEM), payload, start)
+    )(partial, in_vmem(payload), start)
+    from_core = swap(send, "roll", 1)
+    keep = pl.pallas_call(
+        keep_kernel,
+        out_shape=part,
+        in_specs=[vmem, vmem],
+        out_specs=vmem,
+        scratch_shapes=work,
+        compiler_params=pltpu.CompilerParams(vmem_limit_bytes=40 * MIB),
+        cost_estimate=cost,
+        name="keep",
+    )(partial, in_vmem(factor_lanes))
+    return roll_factor, keep, from_core
 
 
 def swap(value, axes, distance):
@@ -284,9 +317,9 @@
     return payload
 
 
-def reduce_blocks(keep, send):
+def reduce_blocks(keep, from_core):
     cross_size = lax.axis_size("cross")
-    value = keep + swap(send, "roll", 1)
+    value = keep + from_core
     mine, his = value[:2], value[2:]
     by_cross = swap(his, "cross", 1)
     by_roll = swap(mine, "roll", 2)
@@ -296,14 +329,20 @@
     return value, swap(value, "roll", 1)
 
 
-def join_kernel(own, other, factor, factor_out, out, sem):
-    core = lax.rem(lax.axis_index("roll"), 2)
-    half = own.shape[0]
-    stores = (
-        pltpu.make_async_copy(own, out.at[pl.ds(pl.multiple_of(core * half, half), half)], sem.at[0]),
-        pltpu.make_async_copy(other, out.at[pl.ds(pl.multiple_of((1 - core) * half, half), half)], sem.at[1]),
-        pltpu.make_async_copy(factor, factor_out, sem.at[2]),
-    )
+def join_kernel(own, other, factor, factor_out, out, whole, sem):
+    core = this_core()
+    bins = own.shape[1]
+    if bins % LANES:
+        both = jnp.concatenate([own[...], other[...]], axis=1)
+        turned = jnp.concatenate([other[...], own[...]], axis=1)
+        whole[...] = jnp.where(core == 0, both, turned)
+        stores = (pltpu.make_async_copy(whole, out, sem.at[0]),)
+    else:
+        stores = (
+            pltpu.make_async_copy(own, out.at[:, pl.ds(pl.multiple_of(core * bins, bins), bins)], sem.at[0]),
+            pltpu.make_async_copy(other, out.at[:, pl.ds(pl.multiple_of((1 - core) * bins, bins), bins)], sem.at[1]),
+        )
+    stores += (pltpu.make_async_copy(factor, factor_out, sem.at[2]),)
     for store in stores:
         store.start()
     for store in stores:
@@ -317,11 +356,14 @@
         join_kernel,
         out_shape=(
             jax.ShapeDtypeStruct(factor.shape, factor.dtype),
-            jax.ShapeDtypeStruct((2 * own.shape[0], own.shape[1]), own.dtype),
+            jax.ShapeDtypeStruct((own.shape[0], 2 * own.shape[1]), own.dtype),
         ),
         in_specs=[vmem, vmem, vmem],
         out_specs=(anywhere, anywhere),
-        scratch_shapes=[pltpu.SemaphoreType.DMA((3,))],
+        scratch_shapes=[
+            pltpu.VMEM((own.shape[0], 2 * own.shape[1]), own.dtype),
+            pltpu.SemaphoreType.DMA((3,)),
+        ],
         compiler_params=pltpu.CompilerParams(vmem_limit_bytes=8 * MIB),
         name="join",
     )(own, other, factor)
@@ -335,8 +377,8 @@
     scale = rank / (all_rolls * all_cross)
     partial_value, payload = stream(density, mach_factor, cross_factor)
     payload = reduce_payload(payload, rank)
-    roll_factor, keep, send = update(scale, partial_value, payload, roll_start)
-    own, other = reduce_blocks(keep, send)
+    roll_factor, keep, from_core = update(scale, partial_value, payload, roll_start)
+    own, other = reduce_blocks(keep, from_core)
     return join(own, other, roll_factor)
 
 

time: 52.1 us -> 51.8 us (level)
  transfers between devices with their start and end apart: 10 -> 10, of which waited for: 10 -> 10; matrix products, arithmetic and copies ran while one was open for 0% -> 0% of each run, Pallas kernels for 0% -> 1%
where the time goes in v5:
time: 51.8 us; the launch traced here: 51.6 us
  Pallas kernels  23.5 us (45%)
  starting transfers between devices  13.7 us (26%)
  waiting for transfers between devices  13.7 us (26%)
  between operations  0.72 us (1%)
    pallas_call x1, Pallas kernels, stream(): pl.pallas_call(stream_kernel, out_shape=(pltpu.VMEM((rolls, span, LANES),...  21.5 us
    ppermute x10, waiting for transfers between devices, swap(): lax.ppermute(value, axes, [(source, source ^ distance) for source in rang...  13.7 us
    ppermute x10, starting transfers between devices, swap(): lax.ppermute(value, axes, [(source, source ^ distance) for source in rang...  13.7 us
  transfers between devices with their start and end apart: 10, of which 10 were waited for; matrix products, arithmetic and copies ran while one was open for 0% of the time, Pallas kernels for 1%

profile of v5, /device:TPU:0, one launch (start us, length us, event | category | flops | bytes accessed | tf_op | source)
XLA Modules:
  0.0 51.6 jit_solution(16049209993710563611)
XLA Ops:
  0.6 21.5 %stream.1 = (f32[32,512,128]{2,1,0:T(8,128)S(1)}, f32[32,128]{1,0:T(8,128)S(1)}) custom-call(bf16[32,2048,512]{2,1,0:T(8,128)(2,1)} %density.1, bf16[32,2048]{1,0:T(8,128)(2,1)} %mach_hbm.1, bf16[32,512]{1,0:T(8,128)(2,1)} %cross_hbm.1), custom_call_target="tpu_custom_call" | custom-call | flops 2147483648 | bytes 67108864 | tf_op jit(solution)/shard_map/stream/pallas_call | solution.py:156
  22.2 4.0 %collective-permute-start.2 = (f32[32,128]{1,0:T(8,128)S(1)}, f32[32,128]{1,0:T(8,128)S(1)}, u32[]{:S(2)}, u32[]{:S(2)}) collective-permute-start(f32[32,128]{1,0:T(8,128)S(1)} %get-tuple-element.8), channel_id=1, source_target_pairs={{0,5},{1,4},{2,7},{3,6},{4,1},{5,0},{6,3},{7,2},{8,13},{9,12},{10,... | collective-permute-start | bytes 49160 | tf_op jit(solution)/shard_map/ppermute | solution.py:288
  26.2 0.5 collective-permute-start.1
  26.6 0.2 collective-permute-start
  26.8 1.1 %collective-permute-done.2 = f32[32,128]{1,0:T(8,128)S(1)} collective-permute-done((f32[32,128]{1,0:T(8,128)S(1)}, f32[32,128]{1,0:T(8,128)S(1)}, u32[]{:S(2)}, u32[]{:S(2)}) %collective-permute-start.2) | collective-permute-done | bytes 16416 | tf_op jit(solution)/shard_map/ppermute | solution.py:288
  27.9 2.0 %collective-permute-done.1 = f32[32,128]{1,0:T(8,128)S(1)} collective-permute-done((f32[32,128]{1,0:T(8,128)S(1)}, f32[32,128]{1,0:T(8,128)S(1)}, u32[]{:S(2)}, u32[]{:S(2)}) %collective-permute-start.1) | collective-permute-done | bytes 16416 | tf_op jit(solution)/shard_map/ppermute | solution.py:288
  29.9 0.5 collective-permute-done
  30.4 2.6 %collective-permute-start.3 = (f32[32,128]{1,0:T(8,128)S(1)}, f32[32,128]{1,0:T(8,128)S(1)}, u32[]{:S(2)}, u32[]{:S(2)}) collective-permute-start(f32[32,128]{1,0:T(8,128)S(1)} %add_add_fusion.1), channel_id=1, source_target_pairs={{0,2},{1,3},{2,0},{3,1},{4,6},{5,7},{6,4},{7,5},{8,10},{9,11},{10,... | collective-permute-start | bytes 49160 | tf_op jit(solution)/shard_map/ppermute | solution.py:288
  33.1 2.0 %collective-permute-done.3 = f32[32,128]{1,0:T(8,128)S(1)} collective-permute-done((f32[32,128]{1,0:T(8,128)S(1)}, f32[32,128]{1,0:T(8,128)S(1)}, u32[]{:S(2)}, u32[]{:S(2)}) %collective-permute-start.3) | collective-permute-done | bytes 16416 | tf_op jit(solution)/shard_map/ppermute | solution.py:288
  35.1 0.9 %update.1 = (f32[32,32]{1,0:T(8,128)S(1)}, f32[32,128]{1,0:T(8,128)S(1)}, f32[4,32,256]{2,1,0:T(8,128)S(1)}) custom-call(f32[32,512,128]{2,1,0:T(8,128)S(1)} %get-tuple-element.7.partial, f32[32,128]{1,0:T(8,128)S(1)} %select_add_fusion.payload, f32[32,32]{1,0:T(8,128)S(1)} %copy-done), custom_call_target="tpu_custom_call" | custom-call | flops 2097152 | tf_op jit(solution)/shard_map/update/pallas_call | solution.py:254
  36.0 0.1 collective-permute-start.4
  36.1 0.4 keep.1
  36.5 0.9 %collective-permute-done.4 = f32[4,32,256]{2,1,0:T(8,128)S(1)} collective-permute-done((f32[4,32,256]{2,1,0:T(8,128)S(1)}, f32[4,32,256]{2,1,0:T(8,128)S(1)}, u32[]{:S(2)}, u32[]{:S(2)}) %collective-permute-start.4) | collective-permute-done | bytes 131104 | tf_op jit(solution)/shard_map/ppermute | solution.py:288
  37.5 1.6 %collective-permute-start.6 = (f32[2,32,256]{2,1,0:T(8,128)S(1)}, f32[2,32,256]{2,1,0:T(8,128)S(1)}, u32[]{:S(2)}, u32[]{:S(2)}) collective-permute-start(f32[2,32,256]{2,1,0:T(8,128)S(1)} %get-tuple-element.12), channel_id=1, source_target_pairs={{0,16},{8,24},{16,0},{24,8},{1,17},{9,25},{17,1},{25,9},{2,18},{10... | collective-permute-start | bytes 196616 | tf_op jit(solution)/shard_map/ppermute | solution.py:288
  39.0 1.5 %collective-permute-start.7 = (f32[2,32,256]{2,1,0:T(8,128)S(1)}, f32[2,32,256]{2,1,0:T(8,128)S(1)}, u32[]{:S(2)}, u32[]{:S(2)}) collective-permute-start(f32[2,32,256]{2,1,0:T(8,128)S(1)} %get-tuple-element.13), channel_id=1, source_target_pairs={{0,17},{1,16},{2,19},{3,18},{8,25},{9,24},{10,27},{11,26},{16,1},{... | collective-permute-start | bytes 196616 | tf_op jit(solution)/shard_map/ppermute | solution.py:288
  40.6 0.5 collective-permute-start.5
  41.0 0.8 %collective-permute-done.6 = f32[2,32,256]{2,1,0:T(8,128)S(1)} collective-permute-done((f32[2,32,256]{2,1,0:T(8,128)S(1)}, f32[2,32,256]{2,1,0:T(8,128)S(1)}, u32[]{:S(2)}, u32[]{:S(2)}) %collective-permute-start.6) | collective-permute-done | bytes 65568 | tf_op jit(solution)/shard_map/ppermute | solution.py:288
  41.8 2.9 %collective-permute-done.7 = f32[2,32,256]{2,1,0:T(8,128)S(1)} collective-permute-done((f32[2,32,256]{2,1,0:T(8,128)S(1)}, f32[2,32,256]{2,1,0:T(8,128)S(1)}, u32[]{:S(2)}, u32[]{:S(2)}) %collective-permute-start.7) | collective-permute-done | bytes 65568 | tf_op jit(solution)/shard_map/ppermute | solution.py:288
  44.7 0.1 collective-permute-done.5
  44.9 2.7 %collective-permute-start.8 = (f32[32,256]{1,0:T(8,128)S(1)}, f32[32,256]{1,0:T(8,128)S(1)}, u32[]{:S(2)}, u32[]{:S(2)}) collective-permute-start(f32[32,256]{1,0:T(8,128)S(1)} %slice_bitcast_fusion), channel_id=1, source_target_pairs={{0,2},{1,3},{2,0},{3,1},{4,6},{5,7},{6,4},{7,5},{8,10},{9,11},{10,... | collective-permute-start | bytes 98312 | tf_op jit(solution)/shard_map/ppermute | solution.py:288
  47.6 2.2 %collective-permute-done.8 = f32[32,256]{1,0:T(8,128)S(1)} collective-permute-done((f32[32,256]{1,0:T(8,128)S(1)}, f32[32,256]{1,0:T(8,128)S(1)}, u32[]{:S(2)}, u32[]{:S(2)}) %collective-permute-start.8) | collective-permute-done | bytes 32800 | tf_op jit(solution)/shard_map/ppermute | solution.py:288
  49.8 0.0 collective-permute-start.9
  49.8 1.2 %collective-permute-done.9.other = f32[32,256]{1,0:T(8,128)S(1)} collective-permute-done((f32[32,256]{1,0:T(8,128)S(1)}, f32[32,256]{1,0:T(8,128)S(1)}, u32[]{:S(2)}, u32[]{:S(2)}) %collective-permute-start.9) | collective-permute-done | bytes 32800 | tf_op jit(solution)/shard_map/ppermute | solution.py:288
  51.0 0.7 %join.1 = (f32[32,32]{1,0:T(8,128)}, f32[32,512]{1,0:T(8,128)}) custom-call(f32[32,256]{1,0:T(8,128)S(1)} %fusion.own, f32[32,256]{1,0:T(8,128)S(1)} %collective-permute-done.9.other, f32[32,32]{1,0:T(8,128)S(1)} %get-tuple-element.11.factor), custom_call_target="tpu_custom_call" | custom-call | tf_op jit(solution)/shard_map/join/pallas_call | solution.py:355
  (12 shorter events, 0.1 us)
Async XLA Ops:
  0.6 34.5 %copy-start = (f32[32,32]{1,0:T(8,128)S(1)}, f32[32,32]{1,0:T(8,128)}, u32[]{:S(2)}) copy-start(f32[32,32]{1,0:T(8,128)} %start.1) | copy-start | bytes 12292
  22.2 5.8 %collective-permute-start.2 = (f32[32,128]{1,0:T(8,128)S(1)}, f32[32,128]{1,0:T(8,128)S(1)}, u32[]{:S(2)}, u32[]{:S(2)}) collective-permute-start(f32[32,128]{1,0:T(8,128)S(1)} %get-tuple-element.8), channel_id=1, source_target_pairs={{0,5},{1,4},{2,7},{3,6},{4,1},{5,0},{6,3},{7,2},{8,13},{9,12},{10,... | collective-permute-start | bytes 49160 | tf_op jit(solution)/shard_map/ppermute | solution.py:288
  26.2 3.7 %collective-permute-start.1 = (f32[32,128]{1,0:T(8,128)S(1)}, f32[32,128]{1,0:T(8,128)S(1)}, u32[]{:S(2)}, u32[]{:S(2)}) collective-permute-start(f32[32,128]{1,0:T(8,128)S(1)} %get-tuple-element.8), channel_id=1, source_target_pairs={{0,1},{1,0},{2,3},{3,2},{4,5},{5,4},{6,7},{7,6},{8,9},{9,8},{10,11... | collective-permute-start | bytes 49160 | tf_op jit(solution)/shard_map/ppermute | solution.py:288
  26.6 3.7 %collective-permute-start = (f32[32,128]{1,0:T(8,128)S(1)}, f32[32,128]{1,0:T(8,128)S(1)}, u32[]{:S(2)}, u32[]{:S(2)}) collective-permute-start(f32[32,128]{1,0:T(8,128)S(1)} %get-tuple-element.8), channel_id=1, source_target_pairs={{0,4},{1,5},{2,6},{3,7},{4,0},{5,1},{6,2},{7,3},{8,12},{9,13},{10,... | collective-permute-start | bytes 49160 | tf_op jit(solution)/shard_map/ppermute | solution.py:288
  30.4 4.7 %collective-permute-start.3 = (f32[32,128]{1,0:T(8,128)S(1)}, f32[32,128]{1,0:T(8,128)S(1)}, u32[]{:S(2)}, u32[]{:S(2)}) collective-permute-start(f32[32,128]{1,0:T(8,128)S(1)} %add_add_fusion.1), channel_id=1, source_target_pairs={{0,2},{1,3},{2,0},{3,1},{4,6},{5,7},{6,4},{7,5},{8,10},{9,11},{10,... | collective-permute-start | bytes 49160 | tf_op jit(solution)/shard_map/ppermute | solution.py:288
  36.0 1.4 %collective-permute-start.4 = (f32[4,32,256]{2,1,0:T(8,128)S(1)}, f32[4,32,256]{2,1,0:T(8,128)S(1)}, u32[]{:S(2)}, u32[]{:S(2)}) collective-permute-start(f32[4,32,256]{2,1,0:T(8,128)S(1)} %get-tuple-element.10), channel_id=1, source_target_pairs={{0,8},{8,0},{16,24},{24,16},{1,9},{9,1},{17,25},{25,17},{2,10},{10... | collective-permute-start | bytes 393224 | tf_op jit(solution)/shard_map/ppermute | solution.py:288
  37.5 4.3 %collective-permute-start.6 = (f32[2,32,256]{2,1,0:T(8,128)S(1)}, f32[2,32,256]{2,1,0:T(8,128)S(1)}, u32[]{:S(2)}, u32[]{:S(2)}) collective-permute-start(f32[2,32,256]{2,1,0:T(8,128)S(1)} %get-tuple-element.12), channel_id=1, source_target_pairs={{0,16},{8,24},{16,0},{24,8},{1,17},{9,25},{17,1},{25,9},{2,18},{10... | collective-permute-start | bytes 196616 | tf_op jit(solution)/shard_map/ppermute | solution.py:288
  39.0 5.7 %collective-permute-start.7 = (f32[2,32,256]{2,1,0:T(8,128)S(1)}, f32[2,32,256]{2,1,0:T(8,128)S(1)}, u32[]{:S(2)}, u32[]{:S(2)}) collective-permute-start(f32[2,32,256]{2,1,0:T(8,128)S(1)} %get-tuple-element.13), channel_id=1, source_target_pairs={{0,17},{1,16},{2,19},{3,18},{8,25},{9,24},{10,27},{11,26},{16,1},{... | collective-permute-start | bytes 196616 | tf_op jit(solution)/shard_map/ppermute | solution.py:288
  40.6 4.3 %collective-permute-start.5 = (f32[2,32,256]{2,1,0:T(8,128)S(1)}, f32[2,32,256]{2,1,0:T(8,128)S(1)}, u32[]{:S(2)}, u32[]{:S(2)}) collective-permute-start(f32[2,32,256]{2,1,0:T(8,128)S(1)} %get-tuple-element.13), channel_id=1, source_target_pairs={{0,1},{1,0},{2,3},{3,2},{4,5},{5,4},{6,7},{7,6},{8,9},{9,8},{10,11... | collective-permute-start | bytes 196616 | tf_op jit(solution)/shard_map/ppermute | solution.py:288
  44.9 4.9 %collective-permute-start.8 = (f32[32,256]{1,0:T(8,128)S(1)}, f32[32,256]{1,0:T(8,128)S(1)}, u32[]{:S(2)}, u32[]{:S(2)}) collective-permute-start(f32[32,256]{1,0:T(8,128)S(1)} %slice_bitcast_fusion), channel_id=1, source_target_pairs={{0,2},{1,3},{2,0},{3,1},{4,6},{5,7},{6,4},{7,5},{8,10},{9,11},{10,... | collective-permute-start | bytes 98312 | tf_op jit(solution)/shard_map/ppermute | solution.py:288
  49.8 1.2 %collective-permute-start.9 = (f32[32,256]{1,0:T(8,128)S(1)}, f32[32,256]{1,0:T(8,128)S(1)}, u32[]{:S(2)}, u32[]{:S(2)}) collective-permute-start(f32[32,256]{1,0:T(8,128)S(1)} %fusion.own), channel_id=1, source_target_pairs={{0,8},{8,0},{16,24},{24,16},{1,9},{9,1},{17,25},{25,17},{2,10},{10... | collective-permute-start | bytes 98312 | tf_op jit(solution)/shard_map/ppermute | solution.py:288

commit v6 on v5

--- a/solution.py
+++ b/solution.py
@@ -198,8 +198,10 @@
         out[slot] = blocks[cross_at ^ distance]
 
 
-def this_core():
-    return lax.rem(lax.axis_index("roll"), 2)
+def this_half():
+    chip, core = lax.axis_index("roll") // 2, lax.rem(lax.axis_index("roll"), 2)
+    cross_at = lax.axis_index("cross")
+    return core ^ chip ^ lax.rem(cross_at, 2) ^ (cross_at // 2)
 
 
 def update_kernel(
@@ -232,11 +234,11 @@
     roll_out[...] = factor
     factor_lanes = jnp.concatenate([factor * scale] * groups, axis=0).T
     lanes_out[...] = factor_lanes
-    half_term(partial, factor_lanes, 1 - this_core(), send, total, blocks)
+    half_term(partial, factor_lanes, 1 - this_half(), send, total, blocks)
 
 
 def keep_kernel(partial, factor_lanes, keep, total, blocks):
-    half_term(partial, factor_lanes[...], this_core(), keep, total, blocks)
+    half_term(partial, factor_lanes[...], this_half(), keep, total, blocks)
 
 
 def update(scale, partial, payload, start):
@@ -321,16 +323,16 @@
     cross_size = lax.axis_size("cross")
     value = keep + from_core
     mine, his = value[:2], value[2:]
-    by_cross = swap(his, "cross", 1)
-    by_roll = swap(mine, "roll", 2)
+    by_cross = swap(his, ("roll", "cross"), 1 * cross_size + 1)
+    by_roll = swap(mine, "roll", 3)
     by_both = swap(his, ("roll", "cross"), 2 * cross_size + 1)
     value = mine + (by_cross + (by_roll + by_both))
-    value = value[0] + swap(value[1], "cross", 2)
+    value = value[0] + swap(value[1], ("roll", "cross"), 1 * cross_size + 2)
     return value, swap(value, "roll", 1)
 
 
 def join_kernel(own, other, factor, factor_out, out, whole, sem):
-    core = this_core()
+    core = this_half()
     bins = own.shape[1]
     if bins % LANES:
         both = jnp.concatenate([own[...], other[...]], axis=1)

time: 51.8 us -> 50.9 us (0.983)
  starting transfers between devices: 13.7 us -> 13 us
    ppermute x10, starting transfers between devices: 13.7 us -> 13 us  [swap(): lax.ppermute(value, axes, [(source, source ^ distance) for source in rang...]
where the time goes in v6:
time: 50.9 us; the launch traced here: 50.7 us
  Pallas kernels  23.5 us (46%)
  waiting for transfers between devices  13.5 us (27%)
  starting transfers between devices  13 us (26%)
  between operations  0.71 us (1%)
    pallas_call x1, Pallas kernels, stream(): pl.pallas_call(stream_kernel, out_shape=(pltpu.VMEM((rolls, span, LANES),...  21.5 us
    ppermute x10, waiting for transfers between devices, swap(): lax.ppermute(value, axes, [(source, source ^ distance) for source in rang...  13.5 us
    ppermute x10, starting transfers between devices, swap(): lax.ppermute(value, axes, [(source, source ^ distance) for source in rang...  13 us
  transfers between devices with their start and end apart: 10, of which 10 were waited for; matrix products, arithmetic and copies ran while one was open for 0% of the time, Pallas kernels for 1%

profile of v6, /device:TPU:0, one launch (start us, length us, event | category | flops | bytes accessed | tf_op | source)
XLA Modules:
  0.0 50.7 jit_solution(5991260218659464632)
XLA Ops:
  0.6 21.5 %stream.1 = (f32[32,512,128]{2,1,0:T(8,128)S(1)}, f32[32,128]{1,0:T(8,128)S(1)}) custom-call(bf16[32,2048,512]{2,1,0:T(8,128)(2,1)} %density.1, bf16[32,2048]{1,0:T(8,128)(2,1)} %mach_hbm.1, bf16[32,512]{1,0:T(8,128)(2,1)} %cross_hbm.1), custom_call_target="tpu_custom_call" | custom-call | flops 2147483648 | bytes 67108864 | tf_op jit(solution)/shard_map/stream/pallas_call | solution.py:156
  22.2 4.0 %collective-permute-start.2 = (f32[32,128]{1,0:T(8,128)S(1)}, f32[32,128]{1,0:T(8,128)S(1)}, u32[]{:S(2)}, u32[]{:S(2)}) collective-permute-start(f32[32,128]{1,0:T(8,128)S(1)} %get-tuple-element.8), channel_id=1, source_target_pairs={{0,5},{1,4},{2,7},{3,6},{4,1},{5,0},{6,3},{7,2},{8,13},{9,12},{10,... | collective-permute-start | bytes 49160 | tf_op jit(solution)/shard_map/ppermute | solution.py:290
  26.2 0.5 collective-permute-start.1
  26.6 0.2 collective-permute-start
  26.8 1.1 %collective-permute-done.2 = f32[32,128]{1,0:T(8,128)S(1)} collective-permute-done((f32[32,128]{1,0:T(8,128)S(1)}, f32[32,128]{1,0:T(8,128)S(1)}, u32[]{:S(2)}, u32[]{:S(2)}) %collective-permute-start.2) | collective-permute-done | bytes 16416 | tf_op jit(solution)/shard_map/ppermute | solution.py:290
  27.9 2.0 %collective-permute-done.1 = f32[32,128]{1,0:T(8,128)S(1)} collective-permute-done((f32[32,128]{1,0:T(8,128)S(1)}, f32[32,128]{1,0:T(8,128)S(1)}, u32[]{:S(2)}, u32[]{:S(2)}) %collective-permute-start.1) | collective-permute-done | bytes 16416 | tf_op jit(solution)/shard_map/ppermute | solution.py:290
  29.9 0.5 collective-permute-done
  30.4 2.6 %collective-permute-start.3 = (f32[32,128]{1,0:T(8,128)S(1)}, f32[32,128]{1,0:T(8,128)S(1)}, u32[]{:S(2)}, u32[]{:S(2)}) collective-permute-start(f32[32,128]{1,0:T(8,128)S(1)} %add_add_fusion.1), channel_id=1, source_target_pairs={{0,2},{1,3},{2,0},{3,1},{4,6},{5,7},{6,4},{7,5},{8,10},{9,11},{10,... | collective-permute-start | bytes 49160 | tf_op jit(solution)/shard_map/ppermute | solution.py:290
  33.1 2.0 %collective-permute-done.3 = f32[32,128]{1,0:T(8,128)S(1)} collective-permute-done((f32[32,128]{1,0:T(8,128)S(1)}, f32[32,128]{1,0:T(8,128)S(1)}, u32[]{:S(2)}, u32[]{:S(2)}) %collective-permute-start.3) | collective-permute-done | bytes 16416 | tf_op jit(solution)/shard_map/ppermute | solution.py:290
  35.1 0.9 %update.1 = (f32[32,32]{1,0:T(8,128)S(1)}, f32[32,128]{1,0:T(8,128)S(1)}, f32[4,32,256]{2,1,0:T(8,128)S(1)}) custom-call(f32[32,512,128]{2,1,0:T(8,128)S(1)} %get-tuple-element.7.partial, f32[32,128]{1,0:T(8,128)S(1)} %select_add_fusion.payload, f32[32,32]{1,0:T(8,128)S(1)} %copy-done), custom_call_target="tpu_custom_call" | custom-call | flops 2097152 | tf_op jit(solution)/shard_map/update/pallas_call | solution.py:256
  36.0 0.1 collective-permute-start.4
  36.1 0.4 keep.1
  36.5 0.9 %collective-permute-done.4 = f32[4,32,256]{2,1,0:T(8,128)S(1)} collective-permute-done((f32[4,32,256]{2,1,0:T(8,128)S(1)}, f32[4,32,256]{2,1,0:T(8,128)S(1)}, u32[]{:S(2)}, u32[]{:S(2)}) %collective-permute-start.4) | collective-permute-done | bytes 131104 | tf_op jit(solution)/shard_map/ppermute | solution.py:290
  37.5 1.3 %collective-permute-start.6 = (f32[2,32,256]{2,1,0:T(8,128)S(1)}, f32[2,32,256]{2,1,0:T(8,128)S(1)}, u32[]{:S(2)}, u32[]{:S(2)}) collective-permute-start(f32[2,32,256]{2,1,0:T(8,128)S(1)} %get-tuple-element.12), channel_id=1, source_target_pairs={{0,24},{8,16},{16,8},{24,0},{1,25},{9,17},{17,9},{25,1},{2,26},{10... | collective-permute-start | bytes 196616 | tf_op jit(solution)/shard_map/ppermute | solution.py:290
  38.8 1.6 %collective-permute-start.7 = (f32[2,32,256]{2,1,0:T(8,128)S(1)}, f32[2,32,256]{2,1,0:T(8,128)S(1)}, u32[]{:S(2)}, u32[]{:S(2)}) collective-permute-start(f32[2,32,256]{2,1,0:T(8,128)S(1)} %get-tuple-element.13), channel_id=1, source_target_pairs={{0,17},{1,16},{2,19},{3,18},{8,25},{9,24},{10,27},{11,26},{16,1},{... | collective-permute-start | bytes 196616 | tf_op jit(solution)/shard_map/ppermute | solution.py:290
  40.4 0.1 collective-permute-start.5
  40.5 1.1 %collective-permute-done.6 = f32[2,32,256]{2,1,0:T(8,128)S(1)} collective-permute-done((f32[2,32,256]{2,1,0:T(8,128)S(1)}, f32[2,32,256]{2,1,0:T(8,128)S(1)}, u32[]{:S(2)}, u32[]{:S(2)}) %collective-permute-start.6) | collective-permute-done | bytes 65568 | tf_op jit(solution)/shard_map/ppermute | solution.py:290
  41.6 2.4 %collective-permute-done.7 = f32[2,32,256]{2,1,0:T(8,128)S(1)} collective-permute-done((f32[2,32,256]{2,1,0:T(8,128)S(1)}, f32[2,32,256]{2,1,0:T(8,128)S(1)}, u32[]{:S(2)}, u32[]{:S(2)}) %collective-permute-start.7) | collective-permute-done | bytes 65568 | tf_op jit(solution)/shard_map/ppermute | solution.py:290
  44.1 0.4 collective-permute-done.5
  44.5 2.4 %collective-permute-start.8 = (f32[32,256]{1,0:T(8,128)S(1)}, f32[32,256]{1,0:T(8,128)S(1)}, u32[]{:S(2)}, u32[]{:S(2)}) collective-permute-start(f32[32,256]{1,0:T(8,128)S(1)} %slice_bitcast_fusion), channel_id=1, source_target_pairs={{0,10},{1,11},{2,8},{3,9},{8,2},{9,3},{10,0},{11,1},{16,26},{17,27... | collective-permute-start | bytes 98312 | tf_op jit(solution)/shard_map/ppermute | solution.py:290
  47.0 1.9 %collective-permute-done.8 = f32[32,256]{1,0:T(8,128)S(1)} collective-permute-done((f32[32,256]{1,0:T(8,128)S(1)}, f32[32,256]{1,0:T(8,128)S(1)}, u32[]{:S(2)}, u32[]{:S(2)}) %collective-permute-start.8) | collective-permute-done | bytes 32800 | tf_op jit(solution)/shard_map/ppermute | solution.py:290
  48.9 0.1 collective-permute-start.9
  49.0 1.1 %collective-permute-done.9.other = f32[32,256]{1,0:T(8,128)S(1)} collective-permute-done((f32[32,256]{1,0:T(8,128)S(1)}, f32[32,256]{1,0:T(8,128)S(1)}, u32[]{:S(2)}, u32[]{:S(2)}) %collective-permute-start.9) | collective-permute-done | bytes 32800 | tf_op jit(solution)/shard_map/ppermute | solution.py:290
  50.1 0.7 %join.1 = (f32[32,32]{1,0:T(8,128)}, f32[32,512]{1,0:T(8,128)}) custom-call(f32[32,256]{1,0:T(8,128)S(1)} %fusion.own, f32[32,256]{1,0:T(8,128)S(1)} %collective-permute-done.9.other, f32[32,32]{1,0:T(8,128)S(1)} %get-tuple-element.11.factor), custom_call_target="tpu_custom_call" | custom-call | tf_op jit(solution)/shard_map/join/pallas_call | solution.py:357
  (12 shorter events, 0.1 us)
Async XLA Ops:
  0.6 34.5 %copy-start = (f32[32,32]{1,0:T(8,128)S(1)}, f32[32,32]{1,0:T(8,128)}, u32[]{:S(2)}) copy-start(f32[32,32]{1,0:T(8,128)} %start.1) | copy-start | bytes 12292
  22.2 5.8 %collective-permute-start.2 = (f32[32,128]{1,0:T(8,128)S(1)}, f32[32,128]{1,0:T(8,128)S(1)}, u32[]{:S(2)}, u32[]{:S(2)}) collective-permute-start(f32[32,128]{1,0:T(8,128)S(1)} %get-tuple-element.8), channel_id=1, source_target_pairs={{0,5},{1,4},{2,7},{3,6},{4,1},{5,0},{6,3},{7,2},{8,13},{9,12},{10,... | collective-permute-start | bytes 49160 | tf_op jit(solution)/shard_map/ppermute | solution.py:290
  26.2 3.7 %collective-permute-start.1 = (f32[32,128]{1,0:T(8,128)S(1)}, f32[32,128]{1,0:T(8,128)S(1)}, u32[]{:S(2)}, u32[]{:S(2)}) collective-permute-start(f32[32,128]{1,0:T(8,128)S(1)} %get-tuple-element.8), channel_id=1, source_target_pairs={{0,1},{1,0},{2,3},{3,2},{4,5},{5,4},{6,7},{7,6},{8,9},{9,8},{10,11... | collective-permute-start | bytes 49160 | tf_op jit(solution)/shard_map/ppermute | solution.py:290
  26.6 3.7 %collective-permute-start = (f32[32,128]{1,0:T(8,128)S(1)}, f32[32,128]{1,0:T(8,128)S(1)}, u32[]{:S(2)}, u32[]{:S(2)}) collective-permute-start(f32[32,128]{1,0:T(8,128)S(1)} %get-tuple-element.8), channel_id=1, source_target_pairs={{0,4},{1,5},{2,6},{3,7},{4,0},{5,1},{6,2},{7,3},{8,12},{9,13},{10,... | collective-permute-start | bytes 49160 | tf_op jit(solution)/shard_map/ppermute | solution.py:290
  30.4 4.7 %collective-permute-start.3 = (f32[32,128]{1,0:T(8,128)S(1)}, f32[32,128]{1,0:T(8,128)S(1)}, u32[]{:S(2)}, u32[]{:S(2)}) collective-permute-start(f32[32,128]{1,0:T(8,128)S(1)} %add_add_fusion.1), channel_id=1, source_target_pairs={{0,2},{1,3},{2,0},{3,1},{4,6},{5,7},{6,4},{7,5},{8,10},{9,11},{10,... | collective-permute-start | bytes 49160 | tf_op jit(solution)/shard_map/ppermute | solution.py:290
  36.0 1.4 %collective-permute-start.4 = (f32[4,32,256]{2,1,0:T(8,128)S(1)}, f32[4,32,256]{2,1,0:T(8,128)S(1)}, u32[]{:S(2)}, u32[]{:S(2)}) collective-permute-start(f32[4,32,256]{2,1,0:T(8,128)S(1)} %get-tuple-element.10), channel_id=1, source_target_pairs={{0,8},{8,0},{16,24},{24,16},{1,9},{9,1},{17,25},{25,17},{2,10},{10... | collective-permute-start | bytes 393224 | tf_op jit(solution)/shard_map/ppermute | solution.py:290
  37.5 4.1 %collective-permute-start.6 = (f32[2,32,256]{2,1,0:T(8,128)S(1)}, f32[2,32,256]{2,1,0:T(8,128)S(1)}, u32[]{:S(2)}, u32[]{:S(2)}) collective-permute-start(f32[2,32,256]{2,1,0:T(8,128)S(1)} %get-tuple-element.12), channel_id=1, source_target_pairs={{0,24},{8,16},{16,8},{24,0},{1,25},{9,17},{17,9},{25,1},{2,26},{10... | collective-permute-start | bytes 196616 | tf_op jit(solution)/shard_map/ppermute | solution.py:290
  38.8 5.3 %collective-permute-start.7 = (f32[2,32,256]{2,1,0:T(8,128)S(1)}, f32[2,32,256]{2,1,0:T(8,128)S(1)}, u32[]{:S(2)}, u32[]{:S(2)}) collective-permute-start(f32[2,32,256]{2,1,0:T(8,128)S(1)} %get-tuple-element.13), channel_id=1, source_target_pairs={{0,17},{1,16},{2,19},{3,18},{8,25},{9,24},{10,27},{11,26},{16,1},{... | collective-permute-start | bytes 196616 | tf_op jit(solution)/shard_map/ppermute | solution.py:290
  40.4 4.1 %collective-permute-start.5 = (f32[2,32,256]{2,1,0:T(8,128)S(1)}, f32[2,32,256]{2,1,0:T(8,128)S(1)}, u32[]{:S(2)}, u32[]{:S(2)}) collective-permute-start(f32[2,32,256]{2,1,0:T(8,128)S(1)} %get-tuple-element.13), channel_id=1, source_target_pairs={{0,9},{1,8},{2,11},{3,10},{8,1},{9,0},{10,3},{11,2},{16,25},{17,24... | collective-permute-start | bytes 196616 | tf_op jit(solution)/shard_map/ppermute | solution.py:290
  44.5 4.3 %collective-permute-start.8 = (f32[32,256]{1,0:T(8,128)S(1)}, f32[32,256]{1,0:T(8,128)S(1)}, u32[]{:S(2)}, u32[]{:S(2)}) collective-permute-start(f32[32,256]{1,0:T(8,128)S(1)} %slice_bitcast_fusion), channel_id=1, source_target_pairs={{0,10},{1,11},{2,8},{3,9},{8,2},{9,3},{10,0},{11,1},{16,26},{17,27... | collective-permute-start | bytes 98312 | tf_op jit(solution)/shard_map/ppermute | solution.py:290
  48.9 1.2 %collective-permute-start.9 = (f32[32,256]{1,0:T(8,128)S(1)}, f32[32,256]{1,0:T(8,128)S(1)}, u32[]{:S(2)}, u32[]{:S(2)}) collective-permute-start(f32[32,256]{1,0:T(8,128)S(1)} %fusion.own), channel_id=1, source_target_pairs={{0,8},{8,0},{16,24},{24,16},{1,9},{9,1},{17,25},{25,17},{2,10},{10... | collective-permute-start | bytes 98312 | tf_op jit(solution)/shard_map/ppermute | solution.py:290
